TPU v7x, 256 devices: a whole 4x4x8 slice. The times are simulated.
256 devices in a mesh: ang: 32 (over x, y, z_lo), slab: 8 (over z_hi, core).
Axes of the slice: x: 4, y: 4, z: 8 (z_hi: 4, z_lo: 2; z = z_hi * 2 + z_lo), core: 2. Of those that a mesh axis runs over, the one named last changes fastest.
Arguments:
- start_volume: float32 [48, 24, 2048], P('slab'), may hold values from -6 to 6
- measured: float32 [64, 48, 2048], P('ang', 'slab'), may hold values from -6 to 6
- row_shift: int32 [64, 48], P('ang'), may hold values from 0 to 24, as said below
- col_shift: int32 [64, 48], P('ang'), may hold values from -16 to 16, as said below
- col_frac: float32 [64, 48], P('ang'), may hold values from 0 to 1
Outputs:
- new_volume: float32 [48, 24, 2048], P('slab')
- new_residual: float32 [64, 48, 2048], P('ang', 'slab')
- new_direction: float32 [48, 24, 2048], P('slab')
Inputs may be any that keep to these rules, and one draw needn't show every extreme that they name: For each angle, row_shift is monotone over the slices, starts or ends at 0, and some angle spans the whole range. For each angle, col_shift is monotone over the slices; some angle reaches both ends.
All inputs are finite; a program needn't handle non-finite values.
Results may differ from a plain program's by a relative error of at most 0.003.
Values sent between devices are 32-bit elements; how exact they have to be, the bound alone decides.
A program may use at most 192 MiB of HBM per device.

v0:
```python
import jax
import jax.numpy as jnp
from jax import lax
from jax.sharding import PartitionSpec as P

CMAX = 16


def project_core(padded, shifts, columns, fracs, row0, nrows, margin, pcols, width):

    def project_step(total, item):
        plane, drow, dcol, dfrac = item

        def project_single(shift, colv, fracv):
            left = lax.dynamic_slice(
                plane, (margin + row0 - shift, pcols - colv - 1), (nrows, width + 1)
            )
            return (1.0 - fracv) * left[:, 1:] + fracv * left[:, :-1]

        return (total + jax.vmap(project_single)(drow, dcol, dfrac), None)

    init = jnp.zeros((shifts.shape[0], nrows, width), jnp.float32)
    total, unused = lax.scan(project_step, init, (padded, shifts.T, columns.T, fracs.T))
    return total


def backproject_core(padded, shifts, columns, fracs, row0, lines, margin, pcols, width):

    def backproject_step(total, item):
        plane, drow, dcol, dfrac = item

        def backproject_single(shift, colv, fracv):
            right = lax.dynamic_slice(
                plane, (margin + shift - row0, pcols + colv), (lines, width + 1)
            )
            return (1.0 - fracv) * right[:, :-1] + fracv * right[:, 1:]

        return (total + jax.vmap(backproject_single)(drow, dcol, dfrac), None)

    init = jnp.zeros((shifts.shape[1], lines, width), jnp.float32)
    total, unused = lax.scan(backproject_step, init, (padded, shifts, columns, fracs))
    return total


def project(volume, shifts, columns, fracs, row0, nrows, margin):
    pcols = CMAX + 1
    padded = jnp.pad(volume, ((0, 0), (margin, margin), (pcols, pcols)))
    return project_core(padded, shifts, columns, fracs, row0, nrows, margin, pcols, volume.shape[2])


def backproject(rows, shifts, columns, fracs, row0, lines, margin):
    pcols = CMAX + 1
    padded = jnp.pad(rows, ((0, 0), (margin, margin), (pcols, pcols)))
    return backproject_core(
        padded, shifts, columns, fracs, row0, lines, margin, pcols, rows.shape[2]
    )


def data_total(image):
    return lax.psum(jnp.sum(image * image), ("ang", "slab"))


def per_device(start_volume, measured, row_shift, col_shift, col_frac):
    slab_count = lax.axis_size("slab")
    slab_index = lax.axis_index("slab")
    own_slices, lines, width = start_volume.shape
    own_rows = measured.shape[1]
    total_rows = own_rows * slab_count
    first = slab_index * own_slices
    own_shift = lax.dynamic_slice_in_dim(row_shift, first, own_slices, 1)
    own_col = lax.dynamic_slice_in_dim(col_shift, first, own_slices, 1)
    own_frac = lax.dynamic_slice_in_dim(col_frac, first, own_slices, 1)

    def forward(volume):
        partial_rows = project(volume, own_shift, own_col, own_frac, 0, total_rows, total_rows)
        return lax.psum_scatter(partial_rows, "slab", scatter_dimension=1, tiled=True)

    def backward(rows):
        whole_rows = lax.all_gather(rows, "slab", axis=1, tiled=True)
        return backproject(whole_rows, own_shift, own_col, own_frac, 0, lines, total_rows)

    def sum_whole(term):
        summed = lax.psum(term, "ang")
        norm_value = lax.psum(jnp.sum(summed * summed), "slab")
        return (summed, norm_value)

    residual = measured - forward(start_volume)
    term_first = backward(residual)
    direction, gamma = sum_whole(term_first)
    image = forward(direction)
    alpha = gamma / data_total(image)
    new_volume = start_volume + alpha * direction
    new_residual = residual - alpha * image
    term_next = backward(new_residual)
    gradient_next, gamma_next = sum_whole(term_next)
    new_direction = gradient_next + gamma_next / gamma * direction
    return (new_volume, new_residual, new_direction)


def solution(mesh):
    return jax.shard_map(
        per_device,
        mesh=mesh,
        in_specs=(
            P("slab", None, None),
            P("ang", "slab", None),
            P("ang", None),
            P("ang", None),
            P("ang", None),
        ),
        out_specs=(P("slab", None, None), P("ang", "slab", None), P("slab", None, None)),
        check_vma=False,
    )
```

profile of v0, /device:TPU:1, one launch (start us, length us, event | category | flops | bytes accessed | tf_op | source)
XLA Modules:
  0.0 1098.8 jit_solution(6092275123811201)
XLA Ops:
  8.4 4.6 pad.14
  13.0 36.9 %while.69 = (s32[]{:T(128)}, f32[2,48,2048]{2,1,0:T(8,128)S(1)}, f32[6,2]{1,0:T(8,128)S(1)}, f32[6,120,2082]{2,1,0:T(8,128)}, s32[6,2]{1,0:T(8,128)S(1)}, /*inde...) while((s32[]{:T(128)}, f32[2,48,2048]{2,1,0:T(8,128)S(1)}, f32[6,2]{1,0:T(8,128)S(1)}, ...), condition=%wide.region_1.2_spmd.clone, body=%wide.region_0.1_spmd.clone.sunk | while | flops 983067 | bytes 5980440 | solution.py:23
  14.4 4.1 while.76
  20.6 4.1 while.76
  26.7 4.1 while.76
  32.9 4.1 while.76
  39.0 4.1 while.76
  45.2 4.1 while.76
  53.0 76.7 %all-reduce.15.cloned.1.call-done = f32[2,48,2048]{2,0,1:T(2,128)} async-done(((f32[2,48,2048]{2,0,1:T(2,128)}), f32[2,48,2048]{2,0,1:T(2,128)}) %all-reduce.15.cloned.1.call-update) | async-done | bytes 786448
  130.6 17.5 %all_gather.6 = f32[2,48,2048]{2,0,1:T(2,128)S(1)} all-gather(f32[2,6,2048]{2,0,1:T(2,128)S(1)} %dynamic-slice_subtract_fusion), channel_id=1, replica_groups=mesh['ang'=32,'slab'=8] {'slab'}, dimensions={1}, use_global_device_ids=true | all-gather | bytes 884736 | tf_op jit(solution)/shard_map/all_gather | solution.py:79
  150.9 35.7 %while.71 = (s32[]{:T(128)}, f32[6,24,2048]{2,1,0:T(8,128)}, f32[2,6]{1,0:T(2,128)S(1)}, f32[2,144,2082]{2,0,1:T(2,128)}, s32[2,6]{1,0:T(2,128)S(1)}, /*index=5*...) while((s32[]{:T(128)}, f32[6,24,2048]{2,1,0:T(8,128)}, f32[2,6]{1,0:T(2,128)S(1)}, ...), condition=%wide.region_4.5_spmd.clone, body=%wide.region_3.4_spmd.clone.sunk | while | flops 1474631 | bytes 9933896 | solution.py:41
  153.8 12.8 %while.77 = (s32[]{:T(128)}, f32[144,2082]{1,0:T(8,128)S(1)}, s32[6,2]{0,1:T(2,128)S(1)}, f32[6,24,2049]{2,1,0:T(8,128)S(1)}, s32[]{:T(128)}) while((s32[]{:T(128)}, f32[144,2082]{1,0:T(8,128)S(1)}, s32[6,2]{0,1:T(2,128)S(1)}, f32[6,24,2049]{2,1,0:T(8,128)S(1)}, s32[]{:T(128)}) %tuple.271), condition=%wide.while_cond.1, body=%wide.while_body.1.sunk | while | flops 2 | bytes 417901 | solution.py:33
  171.1 12.8 %while.77 = (s32[]{:T(128)}, f32[144,2082]{1,0:T(8,128)S(1)}, s32[6,2]{0,1:T(2,128)S(1)}, f32[6,24,2049]{2,1,0:T(8,128)S(1)}, s32[]{:T(128)}) while((s32[]{:T(128)}, f32[144,2082]{1,0:T(8,128)S(1)}, s32[6,2]{0,1:T(2,128)S(1)}, f32[6,24,2049]{2,1,0:T(8,128)S(1)}, s32[]{:T(128)}) %tuple.271), condition=%wide.while_cond.1, body=%wide.while_body.1.sunk | while | flops 2 | bytes 417901 | solution.py:33
  186.7 288.0 %all-reduce.11.cloned.1.call-done = f32[6,24,2048]{2,1,0:T(8,128)} async-done(((f32[6,24,2048]{2,1,0:T(8,128)}), f32[6,24,2048]{2,1,0:T(8,128)}) %all-reduce.11.cloned.1.call-update) | async-done | bytes 1179664 | tf_op jit(solution)/shard_map/psum | solution.py:83
  474.8 4.6 pad.16
  479.4 36.8 %while.73 = (s32[]{:T(128)}, f32[2,48,2048]{2,1,0:T(8,128)S(1)}, f32[6,2]{1,0:T(8,128)S(1)}, f32[6,120,2082]{2,1,0:T(8,128)}, s32[6,2]{1,0:T(8,128)S(1)}, /*inde...) while((s32[]{:T(128)}, f32[2,48,2048]{2,1,0:T(8,128)S(1)}, f32[6,2]{1,0:T(8,128)S(1)}, ...), condition=%wide.region_9.10_spmd.clone, body=%wide.region_8.9_spmd.clone.sunk | while | flops 983067 | bytes 5980440 | solution.py:23
  480.8 4.1 while.78
  486.9 4.1 while.78
  493.1 4.1 while.78
  499.2 4.1 while.78
  505.3 4.1 while.78
  511.5 4.1 while.78
  518.7 92.8 %all-reduce.17.cloned.1.call-done = f32[2,48,2048]{2,0,1:T(2,128)} async-done(((f32[2,48,2048]{2,0,1:T(2,128)}), f32[2,48,2048]{2,0,1:T(2,128)}) %all-reduce.17.cloned.1.call-update) | async-done | bytes 786448
  613.1 16.2 %psum.36 = f32[]{:T(128)} all-reduce(f32[]{:T(128)} %multiply_reduce_fusion.1), channel_id=1, replica_groups=mesh['ang'=32,'slab'=8] {'slab'}, use_global_device_ids=true, to_apply=%region_7.8 | all-reduce | flops 1 | bytes 8 | tf_op jit(solution)/shard_map/psum | solution.py:84
  629.3 75.8 %psum.37 = f32[]{:T(128)} all-reduce(f32[]{:T(128)} %multiply_reduce_fusion.2), channel_id=1, replica_groups=mesh['ang'=32,'slab'=8] {'ang','slab'}, use_global_device_ids=true, to_apply=%region_12.13 | all-reduce | flops 1 | bytes 8 | tf_op jit(solution)/shard_map/psum | solution.py:60
  707.5 16.5 %all_gather.7 = f32[2,48,2048]{2,0,1:T(2,128)S(1)} all-gather(f32[2,6,2048]{2,0,1:T(2,128)S(1)} %multiply_subtract_fusion), channel_id=1, replica_groups=mesh['ang'=32,'slab'=8] {'slab'}, dimensions={1}, use_global_device_ids=true | all-gather | bytes 884736 | tf_op jit(solution)/shard_map/all_gather | solution.py:79
  726.8 35.6 %while.75 = (s32[]{:T(128)}, f32[6,24,2048]{2,1,0:T(8,128)}, f32[2,6]{1,0:T(2,128)S(1)}, f32[2,144,2082]{2,0,1:T(2,128)}, s32[2,6]{1,0:T(2,128)S(1)}, /*index=5*...) while((s32[]{:T(128)}, f32[6,24,2048]{2,1,0:T(8,128)}, f32[2,6]{1,0:T(2,128)S(1)}, ...), condition=%wide.region_14.15_spmd.clone, body=%wide.region_13.14_spmd.clone.sunk | while | flops 1474631 | bytes 9933896 | solution.py:41
  729.7 12.8 %while.79 = (s32[]{:T(128)}, f32[144,2082]{1,0:T(8,128)S(1)}, s32[6,2]{0,1:T(2,128)S(1)}, f32[6,24,2049]{2,1,0:T(8,128)S(1)}, s32[]{:T(128)}) while((s32[]{:T(128)}, f32[144,2082]{1,0:T(8,128)S(1)}, s32[6,2]{0,1:T(2,128)S(1)}, f32[6,24,2049]{2,1,0:T(8,128)S(1)}, s32[]{:T(128)}) %tuple.272), condition=%wide.while_cond.3, body=%wide.while_body.3.sunk | while | flops 2 | bytes 417901 | solution.py:33
  746.9 12.8 %while.79 = (s32[]{:T(128)}, f32[144,2082]{1,0:T(8,128)S(1)}, s32[6,2]{0,1:T(2,128)S(1)}, f32[6,24,2049]{2,1,0:T(8,128)S(1)}, s32[]{:T(128)}) while((s32[]{:T(128)}, f32[144,2082]{1,0:T(8,128)S(1)}, s32[6,2]{0,1:T(2,128)S(1)}, f32[6,24,2049]{2,1,0:T(8,128)S(1)}, s32[]{:T(128)}) %tuple.272), condition=%wide.while_cond.3, body=%wide.while_body.3.sunk | while | flops 2 | bytes 417901 | solution.py:33
  762.5 287.2 %all-reduce.13.cloned.1.call-done = f32[6,24,2048]{2,1,0:T(8,128)} async-done(((f32[6,24,2048]{2,1,0:T(8,128)}), f32[6,24,2048]{2,1,0:T(8,128)}) %all-reduce.13.cloned.1.call-update) | async-done | bytes 1179664 | tf_op jit(solution)/shard_map/psum | solution.py:83
  1051.9 35.9 %psum.39 = f32[]{:T(128)} all-reduce(f32[]{:T(128)} %multiply_reduce_fusion), channel_id=1, replica_groups=mesh['ang'=32,'slab'=8] {'slab'}, use_global_device_ids=true, to_apply=%region_17.18 | all-reduce | flops 1 | bytes 8 | tf_op jit(solution)/shard_map/psum | solution.py:84
  1089.2 3.0 multiply_add_fusion
  (298 shorter events, 160.5 us)
Async XLA Ops:
  7.2 1.0 copy-start
  7.2 122.5 %all-reduce.15.cloned.1.call-start = ((), (), s32[]{:S(2)}) async-start(), calls=%async_computation.2 | async-start | bytes 1572864
  49.9 1.6 copy-start.6
  49.9 79.7 %copy-start.5 = (f32[2,6,2048]{2,0,1:T(2,128)S(1)}, f32[2,6,2048]{2,0,1:T(2,128)}, u32[]{:S(2)}) copy-start(f32[2,6,2048]{2,0,1:T(2,128)} %param.14) | copy-start | bytes 294916
  51.5 423.3 %all-reduce.11.cloned.1.call-start = ((), (), s32[]{:S(2)}) async-start(), calls=%async_computation | async-start | bytes 2359296 | tf_op jit(solution)/shard_map/psum | solution.py:83
  186.7 424.8 %all-reduce.17.cloned.1.call-start = ((), (), s32[]{:S(2)}) async-start(), calls=%async_computation.3 | async-start | bytes 1572864
  516.2 1.6 copy-start.1
  517.7 532.0 %all-reduce.13.cloned.1.call-start = ((), (), s32[]{:S(2)}) async-start(), calls=%async_computation.1 | async-start | bytes 2359296 | tf_op jit(solution)/shard_map/psum | solution.py:83
  707.5 19.4 %copy-start.4 = (f32[2,6,2048]{2,0,1:T(2,128)}, f32[2,6,2048]{2,0,1:T(2,128)S(1)}, u32[]{:S(2)}) copy-start(f32[2,6,2048]{2,0,1:T(2,128)S(1)} %multiply_subtract_fusion) | copy-start | bytes 294916
  762.5 326.7 %copy-start.2 = (f32[6,24,2048]{2,1,0:T(8,128)S(1)}, f32[6,24,2048]{2,1,0:T(8,128)}, u32[]{:S(2)}) copy-start(f32[6,24,2048]{2,1,0:T(8,128)} %all-reduce.11.cloned.1.call-done) | copy-start | bytes 3538948
  1049.7 39.5 %copy-start.3 = (f32[6,24,2048]{2,1,0:T(8,128)S(1)}, f32[6,24,2048]{2,1,0:T(8,128)}, u32[]{:S(2)}) copy-start(f32[6,24,2048]{2,1,0:T(8,128)} %all-reduce.13.cloned.1.call-done) | copy-start | bytes 3538948
Sparse Core Ops, SparseCore 0:
  51.6 78.0 all-reduce.14
  186.8 287.9 all-reduce.10
  517.8 93.6 all-reduce.16
  762.6 287.0 all-reduce.12
where the time goes:
time: 1100 us
  waiting for transfers between devices  745 us (68%)
  blocking collectives  162 us (15%)
  local copies, waits for them, and re-layouts  147 us (13%)
  other arithmetic  25.1 us (2%)
  between operations  17.4 us (2%)
    psum x2, waiting for transfers between devices, sum_whole(): summed = lax.psum(term, 'ang')  575 us
    unnamed x6, waiting for transfers between devices  170 us
    gather x144, local copies, waits for them, and re-layouts  99.6 us
    psum x1, blocking collectives, data_total(): return lax.psum(jnp.sum(image * image), ('ang', 'slab'))  75.8 us
    psum x2, blocking collectives, sum_whole(): norm_value = lax.psum(jnp.sum(summed * summed), 'slab')  52 us
    all_gather x2, blocking collectives, backward(): whole_rows = lax.all_gather(rows, 'slab', axis=1, tiled=True)  34 us
  transfers between devices with their start and end apart: 4, of which 4 were waited for; matrix products, arithmetic and copies ran while one was open for 0% of the time, Pallas kernels for 0%

commit v1 on v0

v1 whole, which is shorter than its diff:
```python
import jax
import jax.numpy as jnp
from jax import lax
from jax.experimental import pallas as pl
from jax.experimental.pallas import tpu as pltpu
from jax.sharding import PartitionSpec as P

MESH = pl.DeviceIdType.MESH
F32 = jnp.float32
PIECES = 16
SLICES = 3
LINES = 24
ROWS = 48
ANGLES = 4
LANES = 128
X = 2048


def rcopy(src, dst, send, recv, dev):
    return pltpu.make_async_remote_copy(
        src_ref=src, dst_ref=dst, send_sem=send, recv_sem=recv, device_id=dev, device_id_type=MESH
    )


def lanes_of(shape):
    return lax.broadcasted_iota(jnp.int32, shape, len(shape) - 1)


def kernel(
    x_hbm, m_hbm, rt_ref, ct_ref, ft_ref,
    vol_out, res_out, dir_out,
    xv, dirv, gslab, qslab, m_ref, msh, mbuf, rtv, ctv, ftv, rts, cts, fts,
    xbuf, xhalo, gbuf, ghalo, packed, pad, img, wide, diff,
    part, rs1, sum1, rs2, own, qpart, qrs1, qsum1, qland,
    rblk, iblk, rres, ires, tiles, sc1, sc2, sc3,
    loc_sem, tab_send, tab_recv, m_send, m_recv, x_send,
    ag_send, ag_recv, hl_send, hl_recv,
    rs_send, rs_recv, rt_send, rt_recv, own_send, own_recv,
    sl_send, sl_recv, blk_send, blk_recv, sc_send, sc_recv, out_sem,
):
    ang = lax.axis_index("ang")
    slab = lax.axis_index("slab")
    p = lax.div(ang, 2)
    zlo = lax.rem(ang, 2)
    px = lax.div(p, 4)
    py = lax.rem(p, 4)
    zhi = lax.div(slab, 2)
    core = lax.rem(slab, 2)
    z = 2 * zhi + zlo
    c = 2 * z + core
    even = core == 0
    u = jnp.where(even, px, py)
    w = jnp.where(even, py, px)

    def pid(a, b):
        return jnp.where(even, 4 * a + b, 4 * b + a)

    def plane_dev(q):
        return (2 * q + zlo, slab)

    def col_dev(k):
        zz = lax.div(k, 2)
        return (2 * p + lax.rem(zz, 2), 2 * lax.div(zz, 2) + lax.rem(k, 2))

    def turn(v, d, n):
        return lax.rem(v + d, n)

    lane = lanes_of((LINES, LANES))
    lane_r = lanes_of((ROWS, LANES))
    me_dev = (ang, slab)

    def xy(a, b):
        return jnp.where(even, a, b), jnp.where(even, b, a)

    def is_me(dev):
        return jnp.logical_and(dev[0] == ang, dev[1] == slab)

    def apart(dev, then, here):
        pl.when(jnp.logical_not(is_me(dev)))(then)
        pl.when(is_me(dev))(here)

    def owner_dev(xx, yy):
        return (2 * (4 * zhi + 2 * core + lax.rem(yy, 2)) + zlo, 2 * xx + lax.div(yy, 2))

    partner = (2 * p + (1 - zlo), slab)
    yhi = lax.div(py, 2)
    ylo = lax.rem(py, 2)

    mload = pltpu.make_async_copy(m_hbm, m_ref, loc_sem.at[0])
    mload.start()
    tables = ((rt_ref, rtv, rts), (ct_ref, ctv, cts), (ft_ref, ftv, fts))

    def table_copy(n):
        return pltpu.make_async_copy(tables[n][0], tables[n][1].at[zlo], loc_sem.at[4 + n])

    for n in range(3):
        table_copy(n).start()
    xload = pltpu.make_async_copy(x_hbm, xv, loc_sem.at[1])
    xload.start()

    barrier = pltpu.get_barrier_semaphore()

    def greet(dev):
        pl.semaphore_signal(barrier, inc=1, device_id=dev, device_id_type=MESH)

    @pl.loop(1, PIECES)
    def _(d):
        greet(col_dev(turn(c, d, PIECES)))

    for d in range(1, 4):
        greet(plane_dev(pid(turn(u, d, 4), w)))
        greet(plane_dev(pid(u, turn(w, d, 4))))
    for a in range(4):
        greet((2 * pid(a, w) + 1 - zlo, slab))
    mine = 0
    for a in range(4):
        to = owner_dev(*xy(a, w))
        pl.when(jnp.logical_not(is_me(to)))(lambda to=to: greet(to))
        mine = mine + jnp.where(is_me(to), 1, 0)
        at_x, at_y = zhi, 2 * core + ylo
        come = (2 * jnp.where(yhi == 0, 4 * a + at_y, 4 * at_x + a) + zlo, 2 * px + yhi)
        pl.when(jnp.logical_not(is_me(come)))(lambda come=come: greet(come))

    lane6 = lanes_of((6, LANES))
    mload.wait()
    for a in range(2):
        prev = jnp.zeros((6, LANES), F32)
        for t in range(17):
            cur = jnp.zeros((6, LANES), F32)
            if t < 16:
                cur = pltpu.roll(m_ref[:, a, pl.ds(LANES * t, LANES)], 64, 1)
            msh[a, :, pl.ds(LANES * t, LANES)] = jnp.where(lane6 < 64, prev, cur)
            prev = cur

    pad[...] = jnp.zeros_like(pad)
    img[...] = jnp.zeros_like(img)
    pl.semaphore_wait(barrier, 15 + 6 + 4 + 8 - 2 * mine)

    def x_each(act_far, act_here):
        for to in range(4):
            for h in range(3):
                cc = 4 * to + 2 * zlo + (1 if h < 2 else 0)
                half = h if h < 2 else ylo
                k = 4 * zhi + 2 * core + half
                src = x_hbm.at[pl.ds(3 * half, SLICES), :, pl.ds(pl.multiple_of(LANES * cc, LANES), LANES)]
                copy = rcopy(src, xbuf.at[k], x_send.at[to, h], ag_recv.at[0, k], col_dev(cc))
                local = pltpu.make_async_copy(src, xbuf.at[k], ag_recv.at[0, k])

                def act(copy=copy, local=local, cc=cc):
                    apart(col_dev(cc), lambda: act_far(copy), lambda: act_here(local))

                if h < 2:
                    pl.when(lax.rem(zhi, 2) == lax.rem(px, 2))(act)
                else:
                    act()

    x_each(lambda copy: copy.start(), lambda copy: copy.start())

    tabs = []
    for n, (src, dst, _) in enumerate(tables):
        t = rcopy(src, dst.at[zlo], tab_send.at[n], tab_recv.at[n], partner)
        t.start()
        tabs.append(t)

    def m_window(k):
        return msh.at[:, :, pl.ds(pl.multiple_of(LANES * k, LANES), 2 * LANES)]

    def m_copy(d):
        k = turn(c, d, PIECES)
        return rcopy(m_window(k), mbuf.at[c], m_send.at[d], m_recv.at[c], col_dev(k))

    @pl.loop(1, PIECES)
    def _(d):
        m_copy(d).start()

    mbuf[c] = msh[:, :, pl.ds(pl.multiple_of(LANES * c, LANES), 2 * LANES)]

    def step(q):
        return jnp.where(q < 2, q, 5 - q)

    def piece_order(t):
        late = t - 9
        dx = jnp.where(t < 9, step(lax.rem(t, 3)), jnp.where(late < 4, 2, step(late - 4)))
        dy = jnp.where(t < 9, step(lax.div(t, 3)), jnp.where(late < 4, step(late), 2))
        return 4 * turn(px, 4 - dx, 4) + turn(py, 4 - dy, 4)

    def gather_send1(buf, n):
        for d in range(1, 4):
            rcopy(buf.at[p], buf.at[p], ag_send.at[n, d - 1], ag_recv.at[n, p],
                  plane_dev(pid(turn(u, d, 4), w))).start()

    def gather_copy2(buf, n, da, d):
        k = pid(turn(u, 4 - da, 4), w)
        return rcopy(buf.at[k], buf.at[k], ag_send.at[n, 3 + 3 * da + d - 1], ag_recv.at[n, k],
                     plane_dev(pid(u, turn(w, d, 4))))

    def halo_copy(halo, n, k, side):
        to = turn(c, 1 if side == 0 else PIECES - 1, PIECES)
        return rcopy(packed.at[n, k, side], halo.at[k, side], hl_send.at[n, side, k], hl_recv.at[n, side, k], col_dev(to))

    def halo_start(buf, halo, n, k):
        for side in range(2):
            shift = 42 if side == 0 else 0
            v = [pltpu.roll(buf[k, i], shift + 42 * i, 1) if shift + i else buf[k, i] for i in range(SLICES)]
            packed[n, k, side] = jnp.where(lane < 42, v[0], jnp.where(lane < 84, v[1], v[2]))
            halo_copy(halo, n, k, side).start()

    def gather_wait(buf, n, k):
        rcopy(buf.at[k], buf.at[k], ag_send.at[n, 0], ag_recv.at[n, k], partner).wait_recv()

    def project_piece(buf, halo, k):
        for s in range(SLICES):
            mid = pltpu.roll(buf[k, s], 64, 1)
            left = jnp.where(c > 0, pltpu.roll(halo[k, 0], (150 - 42 * s) % LANES, 1), 0.0)
            right = jnp.where(c < PIECES - 1, pltpu.roll(halo[k, 1], (192 - 42 * s) % LANES, 1), 0.0)
            w0 = jnp.where(lane < 64, left, mid)
            w1 = jnp.where(lane < 64, mid, right)
            s0 = pltpu.roll(w0, 1, 1)
            s1 = pltpu.roll(w1, 1, 1)
            d0 = jnp.where(lane < 1, s1, s0) - w0
            d1 = jnp.where(lane < 1, s0, s1) - w1
            at = SLICES * k + s
            for a in range(ANGLES):
                f = fts[a // 2, a % 2, at]
                cs = cts[a // 2, a % 2, at]
                v0 = w0 + f * d0
                v1 = w1 + f * d1
                other = jnp.logical_or(lane >= LANES - cs, lane < -cs)
                sh = lax.rem(cs + LANES, LANES)
                pad[SLICES * a + s, 0, pl.ds(LINES, LINES), :] = pltpu.roll(jnp.where(other, v1, v0), sh, 1)
                pad[SLICES * a + s, 1, pl.ds(LINES, LINES), :] = pltpu.roll(jnp.where(other, v0, v1), sh, 1)
        for a in range(ANGLES):
            for t in range(2):
                acc = img[a, t]
                for s in range(SLICES):
                    rs = rts[a // 2, a % 2, SLICES * k + s]
                    acc = acc + pad[SLICES * a + s, t, pl.ds(LINES - rs, ROWS), :]
                img[a, t] = acc

    def gather_project(buf, halo, n):
        for da in (0, 1, 3, 2):
            k = pid(turn(u, 4 - da, 4), w)
            if n == 0 or da:
                gather_wait(buf, n, k)
            for d in (2, 1, 3) if n else (1, 3):
                gather_copy2(buf, n, da, d).start()
            halo_start(buf, halo, n, k)

        @pl.loop(0, 8)
        def _(t):
            k = pid(turn(u, 4 - step(lax.div(t, 2)), 4), turn(w, 3 - 2 * lax.rem(t, 2), 4))
            gather_wait(buf, n, k)
            halo_start(buf, halo, n, k)

        @pl.loop(0, PIECES)
        def _(t):
            @pl.when(jnp.logical_and(t >= 4, t < 8))
            def _():
                k = pid(turn(u, 4 - step(t - 4), 4), turn(w, 2, 4))
                gather_wait(buf, n, k)
                halo_start(buf, halo, n, k)

            k = piece_order(t)
            for side in range(2):
                halo_copy(halo, n, k, side).wait_recv()
            project_piece(buf, halo, k)

    def col_mask(t, ln):
        if t == 0:
            return jnp.logical_or(ln >= 64, c > 0)
        return jnp.logical_or(ln < 64, c < PIECES - 1)

    def own_tile(v0, v1, ln):
        return pltpu.roll(jnp.where(ln >= 64, v0, v1), 64, 1)

    def make_diff():
        for a in range(ANGLES):
            v0 = wide[a, 0]
            v1 = wide[a, 1]
            s0 = pltpu.roll(v0, LANES - 1, 1)
            s1 = pltpu.roll(v1, LANES - 1, 1)
            diff[a, 0] = jnp.where(lane_r == LANES - 1, s1, s0) - v0
            diff[a, 1] = jnp.where(lane_r == LANES - 1, s0, s1) - v1

    def back_piece(dst, k):
        for s in range(SLICES):
            at = SLICES * k + s
            acc = None
            for a in range(ANGLES):
                rs = rts[a // 2, a % 2, at]
                cs = cts[a // 2, a % 2, at]
                f = fts[a // 2, a % 2, at]
                first = lane >= 64 + cs
                v = jnp.where(first, wide[a, 0, pl.ds(rs, LINES), :], wide[a, 1, pl.ds(rs, LINES), :])
                e = jnp.where(first, diff[a, 0, pl.ds(rs, LINES), :], diff[a, 1, pl.ds(rs, LINES), :])
                term = pltpu.roll(v + f * e, 64 - cs, 1)
                acc = term if acc is None else acc + term
            dst[k, s] = acc

    def scatter_copy1(src, land, n, d, a):
        return rcopy(src.at[pid(a, turn(w, d, 4))], land.at[d - 1, a], rs_send.at[n, 4 * (d - 1) + a],
                     rs_recv.at[n, 4 * (d - 1) + a], plane_dev(pid(u, turn(w, d, 4))))

    def scatter_copy2(src, dst, n, d):
        a = turn(u, d, 4)
        return rcopy(src.at[a], dst.at[d - 1], rt_send.at[n, d - 1], rt_recv.at[n, d - 1], plane_dev(pid(a, w)))

    def back_scatter(dst, land, n, first):
        @pl.loop(0, PIECES)
        def _(t):
            i = lax.rem(t, 3)
            d = jnp.where(t >= 12, 0, jnp.where(i == 0, 2, 2 * i - 1))
            a = turn(first, jnp.where(t >= 12, t - 12, lax.div(t, 3)), 4)
            back_piece(dst, pid(a, turn(w, d, 4)))

            @pl.when(t < 12)
            def _():
                scatter_copy1(dst, land, n, d, a).start()

    def line_sum(dst, land, n, a):
        total = dst[pid(a, w)]
        for d in (1, 3, 2):
            scatter_copy1(dst, land, n, d, a).wait_recv()
            total = total + land[d - 1, a]
        return total

    def plane_sum(dst, land, total1, land2, n):
        for da in (1, 2, 3, 0):
            a = turn(u, da, 4)
            total1[a] = line_sum(dst, land, n, a)
            if da:
                scatter_copy2(total1, land2, n, da).start()
        total = total1[u]
        for d in (1, 3, 2):
            scatter_copy2(total1, land2, n, d).wait_recv()
            total = total + land2[d - 1]
        return total

    def owner_copy(a, total1, land):
        return rcopy(total1.at[a], land.at[u], own_send.at[a], own_recv.at[u], owner_dev(*xy(a, w)))

    def owner_start(dst, land1, total1, land, n):
        for a in range(4):
            total1[a] = line_sum(dst, land1, n, a)
            copy = owner_copy(a, total1, land)
            local = pltpu.make_async_copy(total1.at[a], land.at[u], own_recv.at[u])
            apart(owner_dev(*xy(a, w)), lambda: copy.start(), lambda: local.start())

    def owner_sum(total1, land):
        total = None
        for a in range(4):
            rcopy(total1.at[0], land.at[a], own_send.at[0], own_recv.at[a], partner).wait_recv()
            total = land[a] if total is None else total + land[a]
        return total

    def owner_finish(total1, land):
        for a in range(4):
            copy = owner_copy(a, total1, land)
            pl.when(jnp.logical_not(is_me(owner_dev(*xy(a, w)))))(lambda: copy.wait_send())

    def slab_at(buf, h, block):
        return buf.at[pl.ds(3 * h, SLICES), :, pl.ds(pl.multiple_of(LANES * block, LANES), LANES)]

    def slab_piece(buf, xx, yy, lo):
        return slab_at(buf, lax.rem(yy, 2), 4 * xx + 2 * lo + lax.div(yy, 2))

    def slab_copy(buf, n, a, b, lo, slot, dev):
        xx, yy = xy(a, b)
        ref = slab_piece(buf, xx, yy, lo)
        return rcopy(ref, ref, sl_send.at[n, slot], sl_recv.at[n, 2 * (4 * xx + yy) + lo], dev)

    def second_dev(d):
        return plane_dev(pid(u, turn(w, d, 4)))

    def slab_wait(buf, n, a, b, lo):
        slab_copy(buf, n, a, b, lo, 0, partner).wait_recv()

    def swap_copy(src, buf, n):
        return rcopy(src, slab_at(buf, ylo, c), sl_send.at[n, 31],
                     sl_recv.at[n, 2 * (4 * zhi + 2 * core + ylo) + zlo], owner_dev(px, py))

    def swap_start(src, buf, n):
        local = pltpu.make_async_copy(src, slab_at(buf, ylo, c), sl_recv.at[n, 2 * (4 * zhi + 2 * core + ylo) + zlo])
        apart(owner_dev(px, py), lambda: swap_copy(src, buf, n).start(), lambda: local.start())

    def slab_near(buf, n, a, lo, slot):
        slab_copy(buf, n, a, w, lo, slot, second_dev(1)).start()
        slab_copy(buf, n, a, w, lo, slot + 1, second_dev(3)).start()

    def slab_first(buf, n):
        for i, d in enumerate((2, 1, 3)):
            slab_copy(buf, n, u, w, zlo, i, plane_dev(pid(turn(u, d, 4), w))).start()
        slab_near(buf, n, u, zlo, 7)
        for i, d in enumerate((2, 1, 3, 0)):
            slab_copy(buf, n, u, w, zlo, 3 + i, (2 * pid(turn(u, d, 4), w) + 1 - zlo, slab)).start()

    def slab_second(buf, n):
        for i, d in enumerate((1, 3, 2)):
            a = turn(u, d, 4)
            slab_wait(buf, n, a, w, zlo)
            slab_near(buf, n, a, zlo, 9 + 2 * i)
        for i, d in enumerate((0, 1, 3, 2)):
            a = turn(u, d, 4)
            slab_wait(buf, n, a, w, 1 - zlo)
            slab_near(buf, n, a, 1 - zlo, 15 + 2 * i)

    def slab_third(buf, n):
        for i, d in enumerate((0, 1, 3, 2)):
            a = turn(u, d, 4)
            slab_wait(buf, n, a, turn(w, 3, 4), 0)
            slab_copy(buf, n, a, turn(w, 3, 4), 0, 23 + 2 * i, second_dev(1)).start()
            slab_wait(buf, n, a, turn(w, 1, 4), 1)
            slab_copy(buf, n, a, turn(w, 1, 4), 1, 24 + 2 * i, second_dev(3)).start()

    def slab_rest(buf, n):
        for lo in range(2):
            for d in (3 if lo else 1, 2):
                @pl.loop(0, 4)
                def _(a):
                    slab_wait(buf, n, a, turn(w, d, 4), lo)

    def slab_finish(buf, n):
        @pl.loop(0, 31)
        def _(t):
            slab_copy(buf, n, u, w, zlo, t, partner).wait_send()

    def blk_copy(src, dst, n, d):
        k = turn(c, d, PIECES)
        return rcopy(src.at[k], dst.at[:, :, pl.ds(pl.multiple_of(LANES * c, LANES), LANES)], blk_send.at[n, d],
                     blk_recv.at[n, c], col_dev(k))

    def blk_send_all(src, dst, n):
        @pl.loop(1, PIECES)
        def _(d):
            blk_copy(src, dst, n, d).start()

        dst[:, :, pl.ds(pl.multiple_of(LANES * c, LANES), LANES)] = src[c]

    def blk_finish(src, dst, n):
        @pl.loop(1, PIECES)
        def _(d):
            k = turn(c, d, PIECES)
            rcopy(src.at[0], dst.at[:, :, pl.ds(pl.multiple_of(LANES * k, LANES), LANES)], blk_send.at[n, d],
                  blk_recv.at[n, k], partner).wait_recv()
            blk_copy(src, dst, n, d).wait_send()

    def gather_finish(buf, halo, n):
        if n:
            for d in range(1, 4):
                rcopy(buf.at[0], buf.at[0], ag_send.at[n, d - 1], ag_recv.at[n, 0], partner).wait_send()
        for da in range(4):
            for d in (1, 2, 3) if n else (1, 3):
                gather_copy2(buf, n, da, d).wait_send()

        @pl.loop(0, PIECES)
        def _(t):
            for side in range(2):
                halo_copy(halo, n, t, side).wait_send()

    def scatter_finish(src, land1, n):
        @pl.loop(0, 12)
        def _(t):
            rcopy(src.at[0], land1.at[0, 0], rs_send.at[n, t], rs_recv.at[n, 0], partner).wait_send()

    def smem_copy(n):
        return pltpu.make_async_copy(tables[n][1], tables[n][2], loc_sem.at[4 + n])

    for n in range(3):
        table_copy(n).wait()
        tabs[n].wait()
        smem_copy(n).start()
    for n in range(3):
        smem_copy(n).wait()

    gather_project(xbuf, xhalo, 0)

    @pl.loop(1, PIECES)
    def _(d):
        k = turn(c, d, PIECES)
        rcopy(m_window(0), mbuf.at[k], m_send.at[d], m_recv.at[k], partner).wait_recv()

    for k in range(PIECES):
        rows = pl.ds(6 * (2 * (k // 4) + k % 2), 6)
        for e in range(2):
            a = 2 * ((k // 2) % 2) + e
            v0 = jnp.where(col_mask(0, lane6), mbuf[k, e, :, :LANES] - img[a, 0, rows, :], 0.0)
            v1 = jnp.where(col_mask(1, lane6), mbuf[k, e, :, LANES:] - img[a, 1, rows, :], 0.0)
            wide[a, 0, rows, :] = v0
            wide[a, 1, rows, :] = v1
            rblk[k, e] = own_tile(v0, v1, lane6)
    make_diff()

    back_scatter(part, rs1, 0, turn(u, 1, 4))
    blk_send_all(rblk, rres, 0)
    own[...] = plane_sum(part, rs1, sum1, rs2, 0)
    gbuf[p] = own[...]
    gather_send1(gbuf, 1)
    swap_start(own, gslab, 0)
    img[...] = jnp.zeros_like(img)
    gather_project(gbuf, ghalo, 1)
    slab_wait(gslab, 0, u, w, zlo)
    slab_first(gslab, 0)

    norm = jnp.zeros((ROWS, LANES), F32)
    for a in range(ANGLES):
        v0 = jnp.where(col_mask(0, lane_r), img[a, 0], 0.0)
        v1 = jnp.where(col_mask(1, lane_r), img[a, 1], 0.0)
        wide[a, 0] = v0
        wide[a, 1] = v1
        mine = jnp.where(lane_r >= 64, v0, v1)
        norm = norm + mine * mine
    make_diff()
    back_scatter(qpart, qrs1, 1, 0)
    slab_second(gslab, 0)
    owner_start(qpart, qrs1, qsum1, qland, 1)
    for k in range(PIECES):
        rows = pl.ds(6 * (2 * (k // 4) + k % 2), 6)
        for e in range(2):
            a = 2 * ((k // 2) % 2) + e
            iblk[k, e] = own_tile(wide[a, 0, rows, :], wide[a, 1, rows, :], lane6)
    q = owner_sum(qsum1, qland)
    qslab[pl.ds(3 * ylo, SLICES), :, pl.ds(pl.multiple_of(LANES * (4 * px + 2 * zlo + yhi), LANES), LANES)] = q
    slab_first(qslab, 1)

    tiles[...] = jnp.zeros_like(tiles)

    def down(v):
        return jnp.sum(v, axis=0, keepdims=True)

    g = own[...]
    tiles[0, 0:1, :] = down(jnp.sum(g * g, axis=0))
    tiles[0, 1:2, :] = down(norm)
    tiles[0, 2:3, :] = down(jnp.sum(q * q, axis=0))

    def sum_copy(land, n, d):
        at, dev = (
            (c, col_dev(turn(c, d, PIECES))),
            (px, plane_dev(4 * turn(px, d, 4) + py)),
            (py, plane_dev(4 * px + turn(py, d, 4))),
        )[n]
        return rcopy(tiles.at[n], land.at[at], sc_send.at[n, d], sc_recv.at[n, at], dev)

    def sum_start(land, n):
        @pl.loop(1, PIECES if n == 0 else 4)
        def _(d):
            sum_copy(land, n, d).start()

        land[(c, px, py)[n]] = tiles[n]

    def sum_finish(land, n):
        count = PIECES if n == 0 else 4

        @pl.loop(1, count)
        def _(d):
            k = turn((c, px, py)[n], d, count)
            rcopy(tiles.at[n], land.at[k], sc_send.at[n, d], sc_recv.at[n, k], partner).wait_recv()
            sum_copy(land, n, d).wait_send()

        total = land[0]
        for k in range(1, count):
            total = total + land[k]
        return total

    sum_start(sc1, 0)
    blk_send_all(iblk, ires, 1)
    slab_third(gslab, 0)
    slab_second(qslab, 1)
    tiles[1] = sum_finish(sc1, 0)
    sum_start(sc2, 1)
    slab_third(qslab, 1)
    tiles[2] = sum_finish(sc2, 1)
    sum_start(sc3, 2)
    slab_rest(gslab, 0)
    sums = jnp.sum(sum_finish(sc3, 2), axis=1, keepdims=True)
    gamma = sums[0:1]
    alpha = gamma / sums[1:2]
    scale = alpha * alpha * (sums[2:3] / gamma)

    blk_finish(rblk, rres, 0)
    blk_finish(iblk, ires, 1)
    for e in range(2):
        res_out[:, e, :] = rres[e] - alpha * ires[e]
    xload.wait()

    def out_copy(src, dst, n, i):
        return pltpu.make_async_copy(src.at[i], dst.at[i], out_sem.at[n, i])

    for i in range(6):
        xv[i] = xv[i] + alpha * gslab[i]
        out_copy(xv, vol_out, 0, i).start()
    slab_rest(qslab, 1)
    for i in range(6):
        dirv[i] = scale * gslab[i] - alpha * qslab[i]
        out_copy(dirv, dir_out, 1, i).start()

    @pl.loop(1, PIECES)
    def _(d):
        m_copy(d).wait_send()

    gather_finish(xbuf, xhalo, 0)
    gather_finish(gbuf, ghalo, 1)
    scatter_finish(part, rs1, 0)
    scatter_finish(qpart, qrs1, 1)
    for d in range(1, 4):
        scatter_copy2(sum1, rs2, 0, d).wait_send()
    owner_finish(qsum1, qland)
    slab_finish(gslab, 0)
    slab_finish(qslab, 1)
    pl.when(jnp.logical_not(is_me(owner_dev(px, py))))(lambda: swap_copy(own, gslab, 0).wait_send())
    x_each(lambda copy: copy.wait_send(), lambda copy: None)
    for i in range(6):
        out_copy(xv, vol_out, 0, i).wait()
        out_copy(dirv, dir_out, 1, i).wait()


def per_device(start_volume, measured, row_shift, col_shift, col_frac):
    piece = (SLICES, LINES, LANES)
    vmem = pltpu.VMEM
    dma = pltpu.SemaphoreType.DMA
    scratch = [
        vmem(start_volume.shape, F32), vmem(start_volume.shape, F32), vmem(start_volume.shape, F32), vmem(start_volume.shape, F32),
        vmem((6, 2, X), F32),
        vmem((2, 6, 17 * LANES), F32),
        vmem((PIECES, 2, 6, 2 * LANES), F32),
        vmem((2, 2, 48), jnp.int32), vmem((2, 2, 48), jnp.int32), vmem((2, 2, 48), F32),
        pltpu.SMEM((2, 2, 48), jnp.int32), pltpu.SMEM((2, 2, 48), jnp.int32), pltpu.SMEM((2, 2, 48), F32),
        vmem((PIECES,) + piece, F32), vmem((PIECES, 2, LINES, LANES), F32),
        vmem((PIECES,) + piece, F32), vmem((PIECES, 2, LINES, LANES), F32),
        vmem((2, PIECES, 2, LINES, LANES), F32),
        vmem((ANGLES * SLICES, 2, 3 * LINES, LANES), F32),
        vmem((ANGLES, 2, ROWS, LANES), F32),
        vmem((ANGLES, 2, ROWS, LANES), F32),
        vmem((ANGLES, 2, ROWS, LANES), F32),
        vmem((PIECES,) + piece, F32), vmem((3, 4) + piece, F32), vmem((4,) + piece, F32), vmem((3,) + piece, F32), vmem(piece, F32),
        vmem((PIECES,) + piece, F32), vmem((3, 4) + piece, F32), vmem((4,) + piece, F32), vmem((4,) + piece, F32),
        vmem((PIECES, 2, 6, LANES), F32), vmem((PIECES, 2, 6, LANES), F32),
        vmem(measured.shape, F32), vmem(measured.shape, F32),
        vmem((3, 8, LANES), F32), vmem((PIECES, 8, LANES), F32), vmem((4, 8, LANES), F32), vmem((4, 8, LANES), F32),
        dma((8,)), dma((3,)), dma((3,)), dma((PIECES,)), dma((PIECES,)), dma((4, 3)),
        dma((2, 15)), dma((2, PIECES)), dma((2, 2, PIECES)), dma((2, 2, PIECES)),
        dma((2, 12)), dma((2, 12)), dma((1, 3)), dma((1, 3)), dma((4,)), dma((4,)),
        dma((2, 32)), dma((2, 32)), dma((2, PIECES)), dma((2, PIECES)), dma((3, PIECES)), dma((3, PIECES)), dma((2, 6)),
    ]
    whole = pl.BlockSpec(memory_space=pltpu.VMEM)
    far = pl.BlockSpec(memory_space=pltpu.HBM)
    rows = jnp.transpose(measured, (1, 0, 2))
    volume, residual, direction = pl.pallas_call(
        kernel,
        out_shape=(
            jax.ShapeDtypeStruct(start_volume.shape, F32),
            jax.ShapeDtypeStruct(rows.shape, F32),
            jax.ShapeDtypeStruct(start_volume.shape, F32),
        ),
        in_specs=[far] * 5,
        out_specs=(far, whole, far),
        scratch_shapes=scratch,
        compiler_params=pltpu.CompilerParams(
            collective_id=0, has_side_effects=True, vmem_limit_bytes=60 * 2**20
        ),
    )(start_volume, rows, row_shift, col_shift, col_frac)
    return volume, jnp.transpose(residual, (1, 0, 2)), direction


def solution(mesh):
    return jax.shard_map(
        per_device,
        mesh=mesh,
        in_specs=(
            P("slab", None, None),
            P("ang", "slab", None),
            P("ang", None),
            P("ang", None),
            P("ang", None),
        ),
        out_specs=(P("slab", None, None), P("ang", "slab", None), P("slab", None, None)),
        check_vma=False,
    )
```

time: 1100 us -> 105 us (0.10)
  waiting for transfers between devices: 745 us -> 0 us
  blocking collectives: 162 us -> 0 us
  local copies, waits for them, and re-layouts: 147 us -> 4.15 us
  Pallas kernels: 0 us -> 100 us
  other arithmetic: 25.1 us -> 0 us
  between operations: 17.4 us -> 0.66 us
    psum x2 -> x0, waiting for transfers between devices: 575 us -> none  [sum_whole(): summed = lax.psum(term, 'ang')]
    unnamed x6 -> x0, waiting for transfers between devices: 170 us -> none
    psum x3 -> x0, blocking collectives: 128 us -> none  [the longest x1 75.8 us: data_total(): return lax.psum(jnp.sum(image * image), ('ang', 'slab'))]
    pallas_call x0 -> x1, Pallas kernels: none -> 100 us  [per_device(): pl.pallas_call(kernel, out_shape=(jax.ShapeDtypeStruct(start_volume.shape...]
    gather x144 -> x0, local copies, waits for them, and re-layouts: 99.6 us -> none
    all_gather x2 -> x0, blocking collectives: 34 us -> none  [backward(): whole_rows = lax.all_gather(rows, 'slab', axis=1, tiled=True)]
    add x17 -> x0, other arithmetic: 17.7 us -> none  [the longest x4 8.31 us: backproject_step(): return (total + jax.vmap(backproject_single)(drow, dcol, dfrac), None)]
    squeeze x12 -> x0, local copies, waits for them, and re-layouts: 15.5 us -> none  [project_core(): lax.scan(project_step, init, (padded, shifts.T, columns.T, fracs.T))]
  transfers between devices with their start and end apart: 4 -> 0, of which waited for: 4 -> 0; matrix products, arithmetic and copies ran while one was open for 0% -> 0% of each run, Pallas kernels for 0% -> 0%
where the time goes in v1:
time: 105 us
  Pallas kernels  100 us (95%)
  local copies, waits for them, and re-layouts  4.15 us (4%)
    pallas_call x1, Pallas kernels, per_device(): pl.pallas_call(kernel, out_shape=(jax.ShapeDtypeStruct(start_volume.shape...  100 us
    unnamed x7, local copies, waits for them, and re-layouts  4.15 us

profile of v1, /device:TPU:1, one launch (start us, length us, event | category | flops | bytes accessed | tf_op | source)
XLA Modules:
  0.0 105.1 jit_solution(9853573404684109694)
XLA Ops:
  0.6 100.3 %shard_map.76 = (f32[6,24,2048]{2,1,0:T(8,128)}, f32[6,2,2048]{2,1,0:T(2,128)}, f32[6,24,2048]{2,1,0:T(8,128)}) custom-call(f32[6,24,2048]{2,1,0:T(8,128)} %x_hbm.1, f32[6,2,2048]{2,1,0:T(2,128)} %bitcast.2, s32[2,48]{1,0:T(2,128)} %rt_ref.1, s32[2,48]{1,0:T(2,128)} %ct_ref.1, f32[2,48]{1,0:T(2,128)} %ft_ref.1), custom_call_target="tpu_custom_call" | custom-call | tf_op jit(solution)/shard_map/pallas_call | solution.py:647
  101.0 0.0 copy-start.1
  101.0 0.0 copy-start
  101.0 2.5 %copy.11 = f32[6,24,2048]{2,1,0:T(8,128)} copy(f32[6,24,2048]{2,1,0:T(8,128)} %get-tuple-element.12) | data formatting | bytes 2359296
  103.5 0.0 copy-done.1
  103.5 0.6 copy.12
  104.1 0.0 copy-done
  104.1 1.0 copy.13
Async XLA Ops:
  101.0 2.5 %copy-start.1 = (f32[6,2,2048]{2,1,0:T(2,128)S(1)}, f32[6,2,2048]{2,1,0:T(2,128)}, u32[]{:S(2)}) copy-start(f32[6,2,2048]{2,1,0:T(2,128)} %get-tuple-element.7) | copy-start | bytes 294916
  101.0 3.1 %copy-start = (f32[6,24,2048]{2,1,0:T(8,128)S(1)}, f32[6,24,2048]{2,1,0:T(8,128)}, u32[]{:S(2)}) copy-start(f32[6,24,2048]{2,1,0:T(8,128)} %get-tuple-element.14) | copy-start | bytes 3538948

commit v2 on v1

--- a/solution.py
+++ b/solution.py
@@ -29,7 +29,7 @@
 def kernel(
     x_hbm, m_hbm, rt_ref, ct_ref, ft_ref,
     vol_out, res_out, dir_out,
-    xv, dirv, gslab, qslab, m_ref, msh, mbuf, rtv, ctv, ftv, rts, cts, fts,
+    xv, volv, dirv, gslab, qslab, m_ref, msh, mbuf, rtv, ctv, ftv, rts, cts, fts,
     xbuf, xhalo, gbuf, ghalo, packed, pad, img, wide, diff,
     part, rs1, sum1, rs2, own, qpart, qrs1, qsum1, qland,
     rblk, iblk, rres, ires, tiles, sc1, sc2, sc3,
@@ -134,6 +134,7 @@
 
     pad[...] = jnp.zeros_like(pad)
     img[...] = jnp.zeros_like(img)
+    xload.wait()
     pl.semaphore_wait(barrier, 15 + 6 + 4 + 8 - 2 * mine)
 
     def x_each(act_far, act_here):
@@ -142,7 +143,7 @@
                 cc = 4 * to + 2 * zlo + (1 if h < 2 else 0)
                 half = h if h < 2 else ylo
                 k = 4 * zhi + 2 * core + half
-                src = x_hbm.at[pl.ds(3 * half, SLICES), :, pl.ds(pl.multiple_of(LANES * cc, LANES), LANES)]
+                src = xv.at[pl.ds(3 * half, SLICES), :, pl.ds(pl.multiple_of(LANES * cc, LANES), LANES)]
                 copy = rcopy(src, xbuf.at[k], x_send.at[to, h], ag_recv.at[0, k], col_dev(cc))
                 local = pltpu.make_async_copy(src, xbuf.at[k], ag_recv.at[0, k])
 
@@ -580,14 +581,13 @@
     blk_finish(iblk, ires, 1)
     for e in range(2):
         res_out[:, e, :] = rres[e] - alpha * ires[e]
-    xload.wait()
 
     def out_copy(src, dst, n, i):
         return pltpu.make_async_copy(src.at[i], dst.at[i], out_sem.at[n, i])
 
     for i in range(6):
-        xv[i] = xv[i] + alpha * gslab[i]
-        out_copy(xv, vol_out, 0, i).start()
+        volv[i] = xv[i] + alpha * gslab[i]
+        out_copy(volv, vol_out, 0, i).start()
     slab_rest(qslab, 1)
     for i in range(6):
         dirv[i] = scale * gslab[i] - alpha * qslab[i]
@@ -609,7 +609,7 @@
     pl.when(jnp.logical_not(is_me(owner_dev(px, py))))(lambda: swap_copy(own, gslab, 0).wait_send())
     x_each(lambda copy: copy.wait_send(), lambda copy: None)
     for i in range(6):
-        out_copy(xv, vol_out, 0, i).wait()
+        out_copy(volv, vol_out, 0, i).wait()
         out_copy(dirv, dir_out, 1, i).wait()
 
 
@@ -618,7 +618,8 @@
     vmem = pltpu.VMEM
     dma = pltpu.SemaphoreType.DMA
     scratch = [
-        vmem(start_volume.shape, F32), vmem(start_volume.shape, F32), vmem(start_volume.shape, F32), vmem(start_volume.shape, F32),
+        vmem(start_volume.shape, F32), vmem(start_volume.shape, F32), vmem(start_volume.shape, F32),
+        vmem(start_volume.shape, F32), vmem(start_volume.shape, F32),
         vmem((6, 2, X), F32),
         vmem((2, 6, 17 * LANES), F32),
         vmem((PIECES, 2, 6, 2 * LANES), F32),

time: 105 us -> 104 us (level)
  Pallas kernels: 100 us -> 98.9 us
    pallas_call x1, Pallas kernels: 100 us -> 98.9 us  [per_device(): pl.pallas_call(kernel, out_shape=(jax.ShapeDtypeStruct(start_volume.shape...]
where the time goes in v2:
time: 104 us
  Pallas kernels  98.9 us (95%)
  local copies, waits for them, and re-layouts  4.15 us (4%)
    pallas_call x1, Pallas kernels, per_device(): pl.pallas_call(kernel, out_shape=(jax.ShapeDtypeStruct(start_volume.shape...  98.9 us
    unnamed x7, local copies, waits for them, and re-layouts  4.15 us

profile of v2, /device:TPU:1, one launch (start us, length us, event | category | flops | bytes accessed | tf_op | source)
XLA Modules:
  0.0 103.7 jit_solution(5696423136220120803)
XLA Ops:
  0.6 98.9 %shard_map.76 = (f32[6,24,2048]{2,1,0:T(8,128)}, f32[6,2,2048]{2,1,0:T(2,128)}, f32[6,24,2048]{2,1,0:T(8,128)}) custom-call(f32[6,24,2048]{2,1,0:T(8,128)} %x_hbm.1, f32[6,2,2048]{2,1,0:T(2,128)} %bitcast.2, s32[2,48]{1,0:T(2,128)} %rt_ref.1, s32[2,48]{1,0:T(2,128)} %ct_ref.1, f32[2,48]{1,0:T(2,128)} %ft_ref.1), custom_call_target="tpu_custom_call" | custom-call | tf_op jit(solution)/shard_map/pallas_call | solution.py:648
  99.5 0.0 copy-start.1
  99.5 0.0 copy-start
  99.5 2.5 %copy.11 = f32[6,24,2048]{2,1,0:T(8,128)} copy(f32[6,24,2048]{2,1,0:T(8,128)} %get-tuple-element.12) | data formatting | bytes 2359296
  102.0 0.0 copy-done.1
  102.0 0.6 copy.12
  102.7 0.0 copy-done
  102.7 1.0 copy.13
Async XLA Ops:
  99.5 2.5 %copy-start.1 = (f32[6,2,2048]{2,1,0:T(2,128)S(1)}, f32[6,2,2048]{2,1,0:T(2,128)}, u32[]{:S(2)}) copy-start(f32[6,2,2048]{2,1,0:T(2,128)} %get-tuple-element.7) | copy-start | bytes 294916
  99.5 3.1 %copy-start = (f32[6,24,2048]{2,1,0:T(8,128)S(1)}, f32[6,24,2048]{2,1,0:T(8,128)}, u32[]{:S(2)}) copy-start(f32[6,24,2048]{2,1,0:T(8,128)} %get-tuple-element.14) | copy-start | bytes 3538948

commit v3 on v2

--- a/solution.py
+++ b/solution.py
@@ -20,6 +20,22 @@
     return pltpu.make_async_remote_copy(
         src_ref=src, dst_ref=dst, send_sem=send, recv_sem=recv, device_id=dev, device_id_type=MESH
     )
+
+
+class Piece:
+    def __init__(self, *args):
+        self.args = args
+
+    def start(self):
+        src, dst, *rest = self.args
+        for i in range(SLICES):
+            rcopy(src.at[i], dst.at[i], *rest).start()
+
+    def wait_send(self):
+        rcopy(*self.args).wait_send()
+
+    def wait_recv(self):
+        rcopy(*self.args).wait_recv()
 
 
 def lanes_of(shape):
@@ -144,7 +160,7 @@
                 half = h if h < 2 else ylo
                 k = 4 * zhi + 2 * core + half
                 src = xv.at[pl.ds(3 * half, SLICES), :, pl.ds(pl.multiple_of(LANES * cc, LANES), LANES)]
-                copy = rcopy(src, xbuf.at[k], x_send.at[to, h], ag_recv.at[0, k], col_dev(cc))
+                copy = Piece(src, xbuf.at[k], x_send.at[to, h], ag_recv.at[0, k], col_dev(cc))
                 local = pltpu.make_async_copy(src, xbuf.at[k], ag_recv.at[0, k])
 
                 def act(copy=copy, local=local, cc=cc):
@@ -187,7 +203,7 @@
 
     def gather_send1(buf, n):
         for d in range(1, 4):
-            rcopy(buf.at[p], buf.at[p], ag_send.at[n, d - 1], ag_recv.at[n, p],
+            Piece(buf.at[p], buf.at[p], ag_send.at[n, d - 1], ag_recv.at[n, p],
                   plane_dev(pid(turn(u, d, 4), w))).start()
 
     def gather_copy2(buf, n, da, d):
@@ -304,7 +320,7 @@
 
     def scatter_copy2(src, dst, n, d):
         a = turn(u, d, 4)
-        return rcopy(src.at[a], dst.at[d - 1], rt_send.at[n, d - 1], rt_recv.at[n, d - 1], plane_dev(pid(a, w)))
+        return Piece(src.at[a], dst.at[d - 1], rt_send.at[n, d - 1], rt_recv.at[n, d - 1], plane_dev(pid(a, w)))
 
     def back_scatter(dst, land, n, first):
         @pl.loop(0, PIECES)
@@ -338,7 +354,7 @@
         return total
 
     def owner_copy(a, total1, land):
-        return rcopy(total1.at[a], land.at[u], own_send.at[a], own_recv.at[u], owner_dev(*xy(a, w)))
+        return Piece(total1.at[a], land.at[u], own_send.at[a], own_recv.at[u], owner_dev(*xy(a, w)))
 
     def owner_start(dst, land1, total1, land, n):
         for a in range(4):
@@ -368,7 +384,7 @@
     def slab_copy(buf, n, a, b, lo, slot, dev):
         xx, yy = xy(a, b)
         ref = slab_piece(buf, xx, yy, lo)
-        return rcopy(ref, ref, sl_send.at[n, slot], sl_recv.at[n, 2 * (4 * xx + yy) + lo], dev)
+        return (Piece if slot < 7 else rcopy)(ref, ref, sl_send.at[n, slot], sl_recv.at[n, 2 * (4 * xx + yy) + lo], dev)
 
     def second_dev(d):
         return plane_dev(pid(u, turn(w, d, 4)))
@@ -423,7 +439,7 @@
     def slab_finish(buf, n):
         @pl.loop(0, 31)
         def _(t):
-            slab_copy(buf, n, u, w, zlo, t, partner).wait_send()
+            rcopy(buf.at[0:3, :, 0:LANES], buf.at[0:3, :, 0:LANES], sl_send.at[n, t], sl_recv.at[n, 0], partner).wait_send()
 
     def blk_copy(src, dst, n, d):
         k = turn(c, d, PIECES)

time: 104 us -> 104 us (level)
  no operation moved by 1% of the time
where the time goes in v3:
time: 104 us
  Pallas kernels  99.2 us (95%)
  local copies, waits for them, and re-layouts  4.15 us (4%)
    pallas_call x1, Pallas kernels, per_device(): pl.pallas_call(kernel, out_shape=(jax.ShapeDtypeStruct(start_volume.shape...  99.2 us
    unnamed x7, local copies, waits for them, and re-layouts  4.15 us

profile of v3, /device:TPU:1, one launch (start us, length us, event | category | flops | bytes accessed | tf_op | source)
XLA Modules:
  0.0 104.0 jit_solution(6644496749946223885)
XLA Ops:
  0.6 99.2 %shard_map.76 = (f32[6,24,2048]{2,1,0:T(8,128)}, f32[6,2,2048]{2,1,0:T(2,128)}, f32[6,24,2048]{2,1,0:T(8,128)}) custom-call(f32[6,24,2048]{2,1,0:T(8,128)} %x_hbm.1, f32[6,2,2048]{2,1,0:T(2,128)} %bitcast.2, s32[2,48]{1,0:T(2,128)} %rt_ref.1, s32[2,48]{1,0:T(2,128)} %ct_ref.1, f32[2,48]{1,0:T(2,128)} %ft_ref.1), custom_call_target="tpu_custom_call" | custom-call | tf_op jit(solution)/shard_map/pallas_call | solution.py:664
  99.8 0.0 copy-start.1
  99.8 0.0 copy-start
  99.8 2.5 %copy.11 = f32[6,24,2048]{2,1,0:T(8,128)} copy(f32[6,24,2048]{2,1,0:T(8,128)} %get-tuple-element.12) | data formatting | bytes 2359296
  102.3 0.0 copy-done.1
  102.3 0.6 copy.12
  103.0 0.0 copy-done
  103.0 1.0 copy.13
Async XLA Ops:
  99.8 2.5 %copy-start.1 = (f32[6,2,2048]{2,1,0:T(2,128)S(1)}, f32[6,2,2048]{2,1,0:T(2,128)}, u32[]{:S(2)}) copy-start(f32[6,2,2048]{2,1,0:T(2,128)} %get-tuple-element.7) | copy-start | bytes 294916
  99.8 3.1 %copy-start = (f32[6,24,2048]{2,1,0:T(8,128)S(1)}, f32[6,24,2048]{2,1,0:T(8,128)}, u32[]{:S(2)}) copy-start(f32[6,24,2048]{2,1,0:T(8,128)} %get-tuple-element.14) | copy-start | bytes 3538948

commit v4 on v2

--- a/solution.py
+++ b/solution.py
@@ -30,7 +30,7 @@
     x_hbm, m_hbm, rt_ref, ct_ref, ft_ref,
     vol_out, res_out, dir_out,
     xv, volv, dirv, gslab, qslab, m_ref, msh, mbuf, rtv, ctv, ftv, rts, cts, fts,
-    xbuf, xhalo, gbuf, ghalo, packed, pad, img, wide, diff,
+    xbuf, xhalo, gbuf, ghalo, pad, img, wide, diff,
     part, rs1, sum1, rs2, own, qpart, qrs1, qsum1, qland,
     rblk, iblk, rres, ires, tiles, sc1, sc2, sc3,
     loc_sem, tab_send, tab_recv, m_send, m_recv, x_send,
@@ -65,8 +65,8 @@
     def turn(v, d, n):
         return lax.rem(v + d, n)
 
-    lane = lanes_of((LINES, LANES))
-    lane_r = lanes_of((ROWS, LANES))
+    lane = lanes_of((8, LANES))
+    exist = jnp.where(lane < 64, jnp.where(c < PIECES - 1, 1, 0), jnp.where(c > 0, 1, 0)) > 0
     me_dev = (ang, slab)
 
     def xy(a, b):
@@ -124,13 +124,12 @@
     lane6 = lanes_of((6, LANES))
     mload.wait()
     for a in range(2):
-        prev = jnp.zeros((6, LANES), F32)
-        for t in range(17):
-            cur = jnp.zeros((6, LANES), F32)
-            if t < 16:
-                cur = pltpu.roll(m_ref[:, a, pl.ds(LANES * t, LANES)], 64, 1)
-            msh[a, :, pl.ds(LANES * t, LANES)] = jnp.where(lane6 < 64, prev, cur)
-            prev = cur
+        for t in range(PIECES):
+            here = m_ref[:, a, pl.ds(LANES * t, LANES)]
+            right = m_ref[:, a, pl.ds(LANES * min(t + 1, 15), LANES)]
+            left = m_ref[:, a, pl.ds(LANES * max(t - 1, 0), LANES)]
+            msh[t, a, :, :LANES] = here
+            msh[t, a, :, LANES:] = jnp.where(lane6 < 64, right, left)
 
     pad[...] = jnp.zeros_like(pad)
     img[...] = jnp.zeros_like(img)
@@ -163,18 +162,15 @@
         t.start()
         tabs.append(t)
 
-    def m_window(k):
-        return msh.at[:, :, pl.ds(pl.multiple_of(LANES * k, LANES), 2 * LANES)]
-
     def m_copy(d):
         k = turn(c, d, PIECES)
-        return rcopy(m_window(k), mbuf.at[c], m_send.at[d], m_recv.at[c], col_dev(k))
+        return rcopy(msh.at[k], mbuf.at[c], m_send.at[d], m_recv.at[c], col_dev(k))
 
     @pl.loop(1, PIECES)
     def _(d):
         m_copy(d).start()
 
-    mbuf[c] = msh[:, :, pl.ds(pl.multiple_of(LANES * c, LANES), 2 * LANES)]
+    mbuf[c] = msh[c]
 
     def step(q):
         return jnp.where(q < 2, q, 5 - q)
@@ -195,29 +191,27 @@
         return rcopy(buf.at[k], buf.at[k], ag_send.at[n, 3 + 3 * da + d - 1], ag_recv.at[n, k],
                      plane_dev(pid(u, turn(w, d, 4))))
 
-    def halo_copy(halo, n, k, side):
+    def halo_copy(buf, halo, n, k, side):
         to = turn(c, 1 if side == 0 else PIECES - 1, PIECES)
-        return rcopy(packed.at[n, k, side], halo.at[k, side], hl_send.at[n, side, k], hl_recv.at[n, side, k], col_dev(to))
+        return rcopy(buf.at[k], halo.at[k, side], hl_send.at[n, side, k], hl_recv.at[n, side, k], col_dev(to))
 
     def halo_start(buf, halo, n, k):
         for side in range(2):
-            shift = 42 if side == 0 else 0
-            v = [pltpu.roll(buf[k, i], shift + 42 * i, 1) if shift + i else buf[k, i] for i in range(SLICES)]
-            packed[n, k, side] = jnp.where(lane < 42, v[0], jnp.where(lane < 84, v[1], v[2]))
-            halo_copy(halo, n, k, side).start()
+            halo_copy(buf, halo, n, k, side).start()
 
     def gather_wait(buf, n, k):
         rcopy(buf.at[k], buf.at[k], ag_send.at[n, 0], ag_recv.at[n, k], partner).wait_recv()
 
+    tiles3 = (SLICES, 8, LANES)
+
     def project_piece(buf, halo, k):
         for s in range(SLICES):
-            mid = pltpu.roll(buf[k, s], 64, 1)
-            left = jnp.where(c > 0, pltpu.roll(halo[k, 0], (150 - 42 * s) % LANES, 1), 0.0)
-            right = jnp.where(c < PIECES - 1, pltpu.roll(halo[k, 1], (192 - 42 * s) % LANES, 1), 0.0)
-            w0 = jnp.where(lane < 64, left, mid)
-            w1 = jnp.where(lane < 64, mid, right)
-            s0 = pltpu.roll(w0, 1, 1)
-            s1 = pltpu.roll(w1, 1, 1)
+            w0 = buf[k, s].reshape(tiles3)
+            left = halo[k, 0, s].reshape(tiles3)
+            right = halo[k, 1, s].reshape(tiles3)
+            w1 = jnp.where(exist, jnp.where(lane < 64, right, left), 0.0)
+            s0 = pltpu.roll(w0, 1, 2)
+            s1 = pltpu.roll(w1, 1, 2)
             d0 = jnp.where(lane < 1, s1, s0) - w0
             d1 = jnp.where(lane < 1, s0, s1) - w1
             at = SLICES * k + s
@@ -228,8 +222,9 @@
                 v1 = w1 + f * d1
                 other = jnp.logical_or(lane >= LANES - cs, lane < -cs)
                 sh = lax.rem(cs + LANES, LANES)
-                pad[SLICES * a + s, 0, pl.ds(LINES, LINES), :] = pltpu.roll(jnp.where(other, v1, v0), sh, 1)
-                pad[SLICES * a + s, 1, pl.ds(LINES, LINES), :] = pltpu.roll(jnp.where(other, v0, v1), sh, 1)
+                full = (LINES, LANES)
+                pad[SLICES * a + s, 0, pl.ds(LINES, LINES), :] = pltpu.roll(jnp.where(other, v1, v0), sh, 2).reshape(full)
+                pad[SLICES * a + s, 1, pl.ds(LINES, LINES), :] = pltpu.roll(jnp.where(other, v0, v1), sh, 2).reshape(full)
         for a in range(ANGLES):
             for t in range(2):
                 acc = img[a, t]
@@ -238,7 +233,7 @@
                     acc = acc + pad[SLICES * a + s, t, pl.ds(LINES - rs, ROWS), :]
                 img[a, t] = acc
 
-    def gather_project(buf, halo, n):
+    def gather_project(buf, halo, n, during):
         for da in (0, 1, 3, 2):
             k = pid(turn(u, 4 - da, 4), w)
             if n == 0 or da:
@@ -255,6 +250,9 @@
 
         @pl.loop(0, PIECES)
         def _(t):
+            if during is not None:
+                pl.when(t == 10)(during)
+
             @pl.when(jnp.logical_and(t >= 4, t < 8))
             def _():
                 k = pid(turn(u, 4 - step(t - 4), 4), turn(w, 2, 4))
@@ -263,25 +261,21 @@
 
             k = piece_order(t)
             for side in range(2):
-                halo_copy(halo, n, k, side).wait_recv()
+                halo_copy(buf, halo, n, k, side).wait_recv()
             project_piece(buf, halo, k)
 
-    def col_mask(t, ln):
-        if t == 0:
-            return jnp.logical_or(ln >= 64, c > 0)
-        return jnp.logical_or(ln < 64, c < PIECES - 1)
-
-    def own_tile(v0, v1, ln):
-        return pltpu.roll(jnp.where(ln >= 64, v0, v1), 64, 1)
+    def halo_mask(v):
+        return jnp.where(exist, v.reshape(ROWS // 8, 8, LANES), 0.0).reshape(ROWS, LANES)
 
     def make_diff():
+        last = lanes_of((ROWS, LANES)) == LANES - 1
         for a in range(ANGLES):
             v0 = wide[a, 0]
             v1 = wide[a, 1]
             s0 = pltpu.roll(v0, LANES - 1, 1)
             s1 = pltpu.roll(v1, LANES - 1, 1)
-            diff[a, 0] = jnp.where(lane_r == LANES - 1, s1, s0) - v0
-            diff[a, 1] = jnp.where(lane_r == LANES - 1, s0, s1) - v1
+            diff[a, 0] = jnp.where(last, s1, s0) - v0
+            diff[a, 1] = jnp.where(last, s0, s1) - v1
 
     def back_piece(dst, k):
         for s in range(SLICES):
@@ -291,12 +285,16 @@
                 rs = rts[a // 2, a % 2, at]
                 cs = cts[a // 2, a % 2, at]
                 f = fts[a // 2, a % 2, at]
-                first = lane >= 64 + cs
-                v = jnp.where(first, wide[a, 0, pl.ds(rs, LINES), :], wide[a, 1, pl.ds(rs, LINES), :])
-                e = jnp.where(first, diff[a, 0, pl.ds(rs, LINES), :], diff[a, 1, pl.ds(rs, LINES), :])
-                term = pltpu.roll(v + f * e, 64 - cs, 1)
+                other = jnp.logical_or(lane < cs, lane >= LANES + cs)
+
+                def rows_at(ref, t):
+                    return ref[a, t, pl.ds(rs, LINES), :].reshape(tiles3)
+
+                v = jnp.where(other, rows_at(wide, 1), rows_at(wide, 0))
+                e = jnp.where(other, rows_at(diff, 1), rows_at(diff, 0))
+                term = pltpu.roll(v + f * e, lax.rem(LANES - cs, LANES), 2)
                 acc = term if acc is None else acc + term
-            dst[k, s] = acc
+            dst[k, s] = acc.reshape(LINES, LANES)
 
     def scatter_copy1(src, land, n, d, a):
         return rcopy(src.at[pid(a, turn(w, d, 4))], land.at[d - 1, a], rs_send.at[n, 4 * (d - 1) + a],
@@ -456,7 +454,7 @@
         @pl.loop(0, PIECES)
         def _(t):
             for side in range(2):
-                halo_copy(halo, n, t, side).wait_send()
+                halo_copy(buf, halo, n, t, side).wait_send()
 
     def scatter_finish(src, land1, n):
         @pl.loop(0, 12)
@@ -473,52 +471,53 @@
     for n in range(3):
         smem_copy(n).wait()
 
-    gather_project(xbuf, xhalo, 0)
-
-    @pl.loop(1, PIECES)
-    def _(d):
-        k = turn(c, d, PIECES)
-        rcopy(m_window(0), mbuf.at[k], m_send.at[d], m_recv.at[k], partner).wait_recv()
-
-    for k in range(PIECES):
-        rows = pl.ds(6 * (2 * (k // 4) + k % 2), 6)
-        for e in range(2):
-            a = 2 * ((k // 2) % 2) + e
-            v0 = jnp.where(col_mask(0, lane6), mbuf[k, e, :, :LANES] - img[a, 0, rows, :], 0.0)
-            v1 = jnp.where(col_mask(1, lane6), mbuf[k, e, :, LANES:] - img[a, 1, rows, :], 0.0)
-            wide[a, 0, rows, :] = v0
-            wide[a, 1, rows, :] = v1
-            rblk[k, e] = own_tile(v0, v1, lane6)
+    def place_measured():
+        @pl.loop(1, PIECES)
+        def _(d):
+            k = turn(c, d, PIECES)
+            rcopy(msh.at[0], mbuf.at[k], m_send.at[d], m_recv.at[k], partner).wait_recv()
+
+        for k in range(PIECES):
+            rows = pl.ds(6 * (2 * (k // 4) + k % 2), 6)
+            for e in range(2):
+                for t in range(2):
+                    wide[2 * ((k // 2) % 2) + e, t, rows, :] = mbuf[k, e, :, LANES * t:LANES * (t + 1)]
+
+    def rows_of(blk):
+        for k in range(PIECES):
+            rows = pl.ds(6 * (2 * (k // 4) + k % 2), 6)
+            for e in range(2):
+                blk[k, e] = wide[2 * ((k // 2) % 2) + e, 0, rows, :]
+
+    gather_project(xbuf, xhalo, 0, place_measured)
+    for a in range(ANGLES):
+        wide[a, 0] = wide[a, 0] - img[a, 0]
+        wide[a, 1] = halo_mask(wide[a, 1] - img[a, 1])
     make_diff()
 
     back_scatter(part, rs1, 0, turn(u, 1, 4))
+    rows_of(rblk)
     blk_send_all(rblk, rres, 0)
     own[...] = plane_sum(part, rs1, sum1, rs2, 0)
     gbuf[p] = own[...]
     gather_send1(gbuf, 1)
     swap_start(own, gslab, 0)
     img[...] = jnp.zeros_like(img)
-    gather_project(gbuf, ghalo, 1)
+    gather_project(gbuf, ghalo, 1, None)
     slab_wait(gslab, 0, u, w, zlo)
     slab_first(gslab, 0)
 
     norm = jnp.zeros((ROWS, LANES), F32)
     for a in range(ANGLES):
-        v0 = jnp.where(col_mask(0, lane_r), img[a, 0], 0.0)
-        v1 = jnp.where(col_mask(1, lane_r), img[a, 1], 0.0)
-        wide[a, 0] = v0
-        wide[a, 1] = v1
-        mine = jnp.where(lane_r >= 64, v0, v1)
+        mine = img[a, 0]
+        wide[a, 0] = mine
+        wide[a, 1] = halo_mask(img[a, 1])
         norm = norm + mine * mine
     make_diff()
     back_scatter(qpart, qrs1, 1, 0)
     slab_second(gslab, 0)
     owner_start(qpart, qrs1, qsum1, qland, 1)
-    for k in range(PIECES):
-        rows = pl.ds(6 * (2 * (k // 4) + k % 2), 6)
-        for e in range(2):
-            a = 2 * ((k // 2) % 2) + e
-            iblk[k, e] = own_tile(wide[a, 0, rows, :], wide[a, 1, rows, :], lane6)
+    rows_of(iblk)
     q = owner_sum(qsum1, qland)
     qslab[pl.ds(3 * ylo, SLICES), :, pl.ds(pl.multiple_of(LANES * (4 * px + 2 * zlo + yhi), LANES), LANES)] = q
     slab_first(qslab, 1)
@@ -621,13 +620,12 @@
         vmem(start_volume.shape, F32), vmem(start_volume.shape, F32), vmem(start_volume.shape, F32),
         vmem(start_volume.shape, F32), vmem(start_volume.shape, F32),
         vmem((6, 2, X), F32),
-        vmem((2, 6, 17 * LANES), F32),
+        vmem((PIECES, 2, 6, 2 * LANES), F32),
         vmem((PIECES, 2, 6, 2 * LANES), F32),
         vmem((2, 2, 48), jnp.int32), vmem((2, 2, 48), jnp.int32), vmem((2, 2, 48), F32),
         pltpu.SMEM((2, 2, 48), jnp.int32), pltpu.SMEM((2, 2, 48), jnp.int32), pltpu.SMEM((2, 2, 48), F32),
-        vmem((PIECES,) + piece, F32), vmem((PIECES, 2, LINES, LANES), F32),
-        vmem((PIECES,) + piece, F32), vmem((PIECES, 2, LINES, LANES), F32),
-        vmem((2, PIECES, 2, LINES, LANES), F32),
+        vmem((PIECES,) + piece, F32), vmem((PIECES, 2) + piece, F32),
+        vmem((PIECES,) + piece, F32), vmem((PIECES, 2) + piece, F32),
         vmem((ANGLES * SLICES, 2, 3 * LINES, LANES), F32),
         vmem((ANGLES, 2, ROWS, LANES), F32),
         vmem((ANGLES, 2, ROWS, LANES), F32),

time: 104 us -> 104 us (level)
  no operation moved by 1% of the time
where the time goes in v4:
time: 104 us
  Pallas kernels  99.2 us (95%)
  local copies, waits for them, and re-layouts  4.15 us (4%)
    pallas_call x1, Pallas kernels, per_device(): pl.pallas_call(kernel, out_shape=(jax.ShapeDtypeStruct(start_volume.shape...  99.2 us
    unnamed x7, local copies, waits for them, and re-layouts  4.15 us

profile of v4, /device:TPU:1, one launch (start us, length us, event | category | flops | bytes accessed | tf_op | source)
XLA Modules:
  0.0 104.0 jit_solution(4393902578079461608)
XLA Ops:
  0.6 99.2 %shard_map.76 = (f32[6,24,2048]{2,1,0:T(8,128)}, f32[6,2,2048]{2,1,0:T(2,128)}, f32[6,24,2048]{2,1,0:T(8,128)}) custom-call(f32[6,24,2048]{2,1,0:T(8,128)} %x_hbm.1, f32[6,2,2048]{2,1,0:T(2,128)} %bitcast.2, s32[2,48]{1,0:T(2,128)} %rt_ref.1, s32[2,48]{1,0:T(2,128)} %ct_ref.1, f32[2,48]{1,0:T(2,128)} %ft_ref.1), custom_call_target="tpu_custom_call" | custom-call | tf_op jit(solution)/shard_map/pallas_call | solution.py:646
  99.8 0.0 copy-start.1
  99.8 0.0 copy-start
  99.8 2.5 %copy.11 = f32[6,24,2048]{2,1,0:T(8,128)} copy(f32[6,24,2048]{2,1,0:T(8,128)} %get-tuple-element.12) | data formatting | bytes 2359296
  102.3 0.0 copy-done.1
  102.3 0.6 copy.12
  103.0 0.0 copy-done
  103.0 1.0 copy.13
Async XLA Ops:
  99.8 2.5 %copy-start.1 = (f32[6,2,2048]{2,1,0:T(2,128)S(1)}, f32[6,2,2048]{2,1,0:T(2,128)}, u32[]{:S(2)}) copy-start(f32[6,2,2048]{2,1,0:T(2,128)} %get-tuple-element.7) | copy-start | bytes 294916
  99.8 3.1 %copy-start = (f32[6,24,2048]{2,1,0:T(8,128)S(1)}, f32[6,24,2048]{2,1,0:T(8,128)}, u32[]{:S(2)}) copy-start(f32[6,24,2048]{2,1,0:T(8,128)} %get-tuple-element.14) | copy-start | bytes 3538948

commit v5 on v4

--- a/solution.py
+++ b/solution.py
@@ -136,10 +136,13 @@
     xload.wait()
     pl.semaphore_wait(barrier, 15 + 6 + 4 + 8 - 2 * mine)
 
+    near = turn(zhi, 3 + 2 * zlo, 4)
+    served = ((zhi, zlo), (near, 0), (near, 1), (turn(zhi, 2, 4), 1 - zlo))
+
     def x_each(act_far, act_here):
-        for to in range(4):
+        for to, (to_hi, to_lo) in enumerate(served):
             for h in range(3):
-                cc = 4 * to + 2 * zlo + (1 if h < 2 else 0)
+                cc = 4 * to_hi + 2 * to_lo + (1 if h < 2 else 0)
                 half = h if h < 2 else ylo
                 k = 4 * zhi + 2 * core + half
                 src = xv.at[pl.ds(3 * half, SLICES), :, pl.ds(pl.multiple_of(LANES * cc, LANES), LANES)]
@@ -149,10 +152,7 @@
                 def act(copy=copy, local=local, cc=cc):
                     apart(col_dev(cc), lambda: act_far(copy), lambda: act_here(local))
 
-                if h < 2:
-                    pl.when(lax.rem(zhi, 2) == lax.rem(px, 2))(act)
-                else:
-                    act()
+                pl.when(zhi == px if h < 2 else core == yhi)(act)
 
     x_each(lambda copy: copy.start(), lambda copy: copy.start())
 
@@ -166,9 +166,10 @@
         k = turn(c, d, PIECES)
         return rcopy(msh.at[k], mbuf.at[c], m_send.at[d], m_recv.at[c], col_dev(k))
 
-    @pl.loop(1, PIECES)
-    def _(d):
-        m_copy(d).start()
+    def m_start():
+        @pl.loop(1, PIECES)
+        def _(d):
+            m_copy(d).start()
 
     mbuf[c] = msh[c]
 
@@ -238,7 +239,7 @@
             k = pid(turn(u, 4 - da, 4), w)
             if n == 0 or da:
                 gather_wait(buf, n, k)
-            for d in (2, 1, 3) if n else (1, 3):
+            for d in (2, 1, 3):
                 gather_copy2(buf, n, da, d).start()
             halo_start(buf, halo, n, k)
 
@@ -247,6 +248,9 @@
             k = pid(turn(u, 4 - step(lax.div(t, 2)), 4), turn(w, 3 - 2 * lax.rem(t, 2), 4))
             gather_wait(buf, n, k)
             halo_start(buf, halo, n, k)
+
+        if n == 0:
+            m_start()
 
         @pl.loop(0, PIECES)
         def _(t):
@@ -448,7 +452,7 @@
             for d in range(1, 4):
                 rcopy(buf.at[0], buf.at[0], ag_send.at[n, d - 1], ag_recv.at[n, 0], partner).wait_send()
         for da in range(4):
-            for d in (1, 2, 3) if n else (1, 3):
+            for d in (1, 2, 3):
                 gather_copy2(buf, n, da, d).wait_send()
 
         @pl.loop(0, PIECES)
@@ -515,66 +519,82 @@
         norm = norm + mine * mine
     make_diff()
     back_scatter(qpart, qrs1, 1, 0)
+
+    tiles[...] = jnp.zeros_like(tiles)
+
+    def down(v):
+        return jnp.sum(v, axis=0, keepdims=True)
+
+    def sum_copy(set_, n, d):
+        at, dev, land = (
+            (c, col_dev(turn(c, d, PIECES)), sc1),
+            (px, plane_dev(4 * turn(px, d, 4) + py), sc2),
+            (py, plane_dev(4 * px + turn(py, d, 4)), sc3),
+        )[n]
+        return rcopy(tiles.at[set_, n], land.at[set_, at], sc_send.at[set_, n, d], sc_recv.at[set_, n, at], dev)
+
+    def sum_start(set_, n):
+        @pl.loop(1, PIECES if n == 0 else 4)
+        def _(d):
+            sum_copy(set_, n, d).start()
+
+        (sc1, sc2, sc3)[n][set_, (c, px, py)[n]] = tiles[set_, n]
+
+    def sum_finish(set_, n):
+        count = PIECES if n == 0 else 4
+        land = (sc1, sc2, sc3)[n]
+
+        @pl.loop(1, count)
+        def _(d):
+            k = turn((c, px, py)[n], d, count)
+            rcopy(tiles.at[set_, n], land.at[set_, k], sc_send.at[set_, n, d], sc_recv.at[set_, n, k], partner).wait_recv()
+            sum_copy(set_, n, d).wait_send()
+
+        total = land[set_, 0]
+        for k in range(1, count):
+            total = total + land[set_, k]
+        return total
+
+    def sum_step(set_, n):
+        tiles[set_, n + 1] = sum_finish(set_, n)
+        sum_start(set_, n + 1)
+
+    g = gbuf[p]
+    tiles[0, 0, 0:1, :] = down(jnp.sum(g * g, axis=0))
+    tiles[0, 0, 1:2, :] = down(norm)
+    sum_start(0, 0)
     slab_second(gslab, 0)
     owner_start(qpart, qrs1, qsum1, qland, 1)
+    sum_step(0, 0)
     rows_of(iblk)
+
+    @pl.loop(1, PIECES)
+    def _(d):
+        m_copy(d).wait_send()
+
+    gather_finish(xbuf, xhalo, 0)
+    gather_finish(gbuf, ghalo, 1)
+    scatter_finish(part, rs1, 0)
+    for d in range(1, 4):
+        scatter_copy2(sum1, rs2, 0, d).wait_send()
+    x_each(lambda copy: copy.wait_send(), lambda copy: None)
     q = owner_sum(qsum1, qland)
     qslab[pl.ds(3 * ylo, SLICES), :, pl.ds(pl.multiple_of(LANES * (4 * px + 2 * zlo + yhi), LANES), LANES)] = q
     slab_first(qslab, 1)
-
-    tiles[...] = jnp.zeros_like(tiles)
-
-    def down(v):
-        return jnp.sum(v, axis=0, keepdims=True)
-
-    g = own[...]
-    tiles[0, 0:1, :] = down(jnp.sum(g * g, axis=0))
-    tiles[0, 1:2, :] = down(norm)
-    tiles[0, 2:3, :] = down(jnp.sum(q * q, axis=0))
-
-    def sum_copy(land, n, d):
-        at, dev = (
-            (c, col_dev(turn(c, d, PIECES))),
-            (px, plane_dev(4 * turn(px, d, 4) + py)),
-            (py, plane_dev(4 * px + turn(py, d, 4))),
-        )[n]
-        return rcopy(tiles.at[n], land.at[at], sc_send.at[n, d], sc_recv.at[n, at], dev)
-
-    def sum_start(land, n):
-        @pl.loop(1, PIECES if n == 0 else 4)
-        def _(d):
-            sum_copy(land, n, d).start()
-
-        land[(c, px, py)[n]] = tiles[n]
-
-    def sum_finish(land, n):
-        count = PIECES if n == 0 else 4
-
-        @pl.loop(1, count)
-        def _(d):
-            k = turn((c, px, py)[n], d, count)
-            rcopy(tiles.at[n], land.at[k], sc_send.at[n, d], sc_recv.at[n, k], partner).wait_recv()
-            sum_copy(land, n, d).wait_send()
-
-        total = land[0]
-        for k in range(1, count):
-            total = total + land[k]
-        return total
-
-    sum_start(sc1, 0)
+    tiles[1, 0, 0:1, :] = down(jnp.sum(q * q, axis=0))
+    sum_start(1, 0)
     blk_send_all(iblk, ires, 1)
+    sum_step(0, 1)
     slab_third(gslab, 0)
     slab_second(qslab, 1)
-    tiles[1] = sum_finish(sc1, 0)
-    sum_start(sc2, 1)
-    slab_third(qslab, 1)
-    tiles[2] = sum_finish(sc2, 1)
-    sum_start(sc3, 2)
-    slab_rest(gslab, 0)
-    sums = jnp.sum(sum_finish(sc3, 2), axis=1, keepdims=True)
+    sum_step(1, 0)
+    scatter_finish(qpart, qrs1, 1)
+    owner_finish(qsum1, qland)
+    sums = jnp.sum(sum_finish(0, 2), axis=1, keepdims=True)
     gamma = sums[0:1]
     alpha = gamma / sums[1:2]
-    scale = alpha * alpha * (sums[2:3] / gamma)
+    slab_third(qslab, 1)
+    sum_step(1, 1)
 
     blk_finish(rblk, rres, 0)
     blk_finish(iblk, ires, 1)
@@ -584,29 +604,19 @@
     def out_copy(src, dst, n, i):
         return pltpu.make_async_copy(src.at[i], dst.at[i], out_sem.at[n, i])
 
+    slab_rest(gslab, 0)
     for i in range(6):
         volv[i] = xv[i] + alpha * gslab[i]
         out_copy(volv, vol_out, 0, i).start()
+    scale = alpha * alpha * (jnp.sum(sum_finish(1, 2), axis=1, keepdims=True)[0:1] / gamma)
     slab_rest(qslab, 1)
     for i in range(6):
         dirv[i] = scale * gslab[i] - alpha * qslab[i]
         out_copy(dirv, dir_out, 1, i).start()
 
-    @pl.loop(1, PIECES)
-    def _(d):
-        m_copy(d).wait_send()
-
-    gather_finish(xbuf, xhalo, 0)
-    gather_finish(gbuf, ghalo, 1)
-    scatter_finish(part, rs1, 0)
-    scatter_finish(qpart, qrs1, 1)
-    for d in range(1, 4):
-        scatter_copy2(sum1, rs2, 0, d).wait_send()
-    owner_finish(qsum1, qland)
     slab_finish(gslab, 0)
     slab_finish(qslab, 1)
     pl.when(jnp.logical_not(is_me(owner_dev(px, py))))(lambda: swap_copy(own, gslab, 0).wait_send())
-    x_each(lambda copy: copy.wait_send(), lambda copy: None)
     for i in range(6):
         out_copy(volv, vol_out, 0, i).wait()
         out_copy(dirv, dir_out, 1, i).wait()
@@ -634,11 +644,11 @@
         vmem((PIECES,) + piece, F32), vmem((3, 4) + piece, F32), vmem((4,) + piece, F32), vmem((4,) + piece, F32),
         vmem((PIECES, 2, 6, LANES), F32), vmem((PIECES, 2, 6, LANES), F32),
         vmem(measured.shape, F32), vmem(measured.shape, F32),
-        vmem((3, 8, LANES), F32), vmem((PIECES, 8, LANES), F32), vmem((4, 8, LANES), F32), vmem((4, 8, LANES), F32),
+        vmem((2, 3, 8, LANES), F32), vmem((2, PIECES, 8, LANES), F32), vmem((2, 4, 8, LANES), F32), vmem((2, 4, 8, LANES), F32),
         dma((8,)), dma((3,)), dma((3,)), dma((PIECES,)), dma((PIECES,)), dma((4, 3)),
         dma((2, 15)), dma((2, PIECES)), dma((2, 2, PIECES)), dma((2, 2, PIECES)),
         dma((2, 12)), dma((2, 12)), dma((1, 3)), dma((1, 3)), dma((4,)), dma((4,)),
-        dma((2, 32)), dma((2, 32)), dma((2, PIECES)), dma((2, PIECES)), dma((3, PIECES)), dma((3, PIECES)), dma((2, 6)),
+        dma((2, 32)), dma((2, 32)), dma((2, PIECES)), dma((2, PIECES)), dma((2, 3, PIECES)), dma((2, 3, PIECES)), dma((2, 6)),
     ]
     whole = pl.BlockSpec(memory_space=pltpu.VMEM)
     far = pl.BlockSpec(memory_space=pltpu.HBM)

time: 104 us -> 104 us (level)
  no operation moved by 1% of the time
where the time goes in v5:
time: 104 us
  Pallas kernels  99.1 us (95%)
  local copies, waits for them, and re-layouts  4.15 us (4%)
    pallas_call x1, Pallas kernels, per_device(): pl.pallas_call(kernel, out_shape=(jax.ShapeDtypeStruct(start_volume.shape...  99.1 us
    unnamed x7, local copies, waits for them, and re-layouts  4.15 us

profile of v5, /device:TPU:1, one launch (start us, length us, event | category | flops | bytes accessed | tf_op | source)
XLA Modules:
  0.0 103.9 jit_solution(14829659399565291393)
XLA Ops:
  0.6 99.1 %shard_map.76 = (f32[6,24,2048]{2,1,0:T(8,128)}, f32[6,2,2048]{2,1,0:T(2,128)}, f32[6,24,2048]{2,1,0:T(8,128)}) custom-call(f32[6,24,2048]{2,1,0:T(8,128)} %x_hbm.1, f32[6,2,2048]{2,1,0:T(2,128)} %bitcast.2, s32[2,48]{1,0:T(2,128)} %rt_ref.1, s32[2,48]{1,0:T(2,128)} %ct_ref.1, f32[2,48]{1,0:T(2,128)} %ft_ref.1), custom_call_target="tpu_custom_call" | custom-call | tf_op jit(solution)/shard_map/pallas_call | solution.py:656
  99.7 0.0 copy-start.1
  99.7 0.0 copy-start
  99.7 2.5 %copy.11 = f32[6,24,2048]{2,1,0:T(8,128)} copy(f32[6,24,2048]{2,1,0:T(8,128)} %get-tuple-element.12) | data formatting | bytes 2359296
  102.2 0.0 copy-done.1
  102.2 0.6 copy.12
  102.8 0.0 copy-done
  102.9 1.0 copy.13
Async XLA Ops:
  99.7 2.5 %copy-start.1 = (f32[6,2,2048]{2,1,0:T(2,128)S(1)}, f32[6,2,2048]{2,1,0:T(2,128)}, u32[]{:S(2)}) copy-start(f32[6,2,2048]{2,1,0:T(2,128)} %get-tuple-element.7) | copy-start | bytes 294916
  99.7 3.1 %copy-start = (f32[6,24,2048]{2,1,0:T(8,128)S(1)}, f32[6,24,2048]{2,1,0:T(8,128)}, u32[]{:S(2)}) copy-start(f32[6,24,2048]{2,1,0:T(8,128)} %get-tuple-element.14) | copy-start | bytes 3538948

commit v6 on v5

--- a/solution.py
+++ b/solution.py
@@ -33,7 +33,7 @@
     xbuf, xhalo, gbuf, ghalo, pad, img, wide, diff,
     part, rs1, sum1, rs2, own, qpart, qrs1, qsum1, qland,
     rblk, iblk, rres, ires, tiles, sc1, sc2, sc3,
-    loc_sem, tab_send, tab_recv, m_send, m_recv, x_send,
+    loc_sem, tab_send, tab_recv, tab_loc, m_send, m_recv, x_send,
     ag_send, ag_recv, hl_send, hl_recv,
     rs_send, rs_recv, rt_send, rt_recv, own_send, own_recv,
     sl_send, sl_recv, blk_send, blk_recv, sc_send, sc_recv, out_sem,
@@ -86,17 +86,10 @@
     yhi = lax.div(py, 2)
     ylo = lax.rem(py, 2)
 
-    mload = pltpu.make_async_copy(m_hbm, m_ref, loc_sem.at[0])
-    mload.start()
     tables = ((rt_ref, rtv, rts), (ct_ref, ctv, cts), (ft_ref, ftv, fts))
 
     def table_copy(n):
-        return pltpu.make_async_copy(tables[n][0], tables[n][1].at[zlo], loc_sem.at[4 + n])
-
-    for n in range(3):
-        table_copy(n).start()
-    xload = pltpu.make_async_copy(x_hbm, xv, loc_sem.at[1])
-    xload.start()
+        return pltpu.make_async_copy(tables[n][0], tables[n][2].at[zlo], loc_sem.at[4 + n])
 
     barrier = pltpu.get_barrier_semaphore()
 
@@ -121,6 +114,44 @@
         come = (2 * jnp.where(yhi == 0, 4 * a + at_y, 4 * at_x + a) + zlo, 2 * px + yhi)
         pl.when(jnp.logical_not(is_me(come)))(lambda come=come: greet(come))
 
+    mload = pltpu.make_async_copy(m_hbm, m_ref, loc_sem.at[0])
+    mload.start()
+    for n in range(3):
+        table_copy(n).start()
+    xload = pltpu.make_async_copy(x_hbm, xv, loc_sem.at[1])
+    xload.start()
+
+    pad[...] = jnp.zeros_like(pad)
+    img[...] = jnp.zeros_like(img)
+    xload.wait()
+    pl.semaphore_wait(barrier, 15 + 6 + 4 + 8 - 2 * mine)
+
+    tabs = []
+    for n, (src, dst, _) in enumerate(tables):
+        t = rcopy(src, dst, tab_send.at[n], tab_recv.at[n], partner)
+        t.start()
+        tabs.append(t)
+
+    near = turn(zhi, 3 + 2 * zlo, 4)
+    served = ((zhi, zlo), (near, 0), (near, 1), (turn(zhi, 2, 4), 1 - zlo))
+
+    def x_each(act_far, act_here):
+        for to, (to_hi, to_lo) in enumerate(served):
+            for h in range(3):
+                cc = 4 * to_hi + 2 * to_lo + (1 if h < 2 else 0)
+                half = h if h < 2 else ylo
+                k = 4 * zhi + 2 * core + half
+                src = xv.at[pl.ds(3 * half, SLICES), :, pl.ds(pl.multiple_of(LANES * cc, LANES), LANES)]
+                copy = rcopy(src, xbuf.at[k], x_send.at[to, h], ag_recv.at[0, k], col_dev(cc))
+                local = pltpu.make_async_copy(src, xbuf.at[k], ag_recv.at[0, k])
+
+                def act(copy=copy, local=local, cc=cc):
+                    apart(col_dev(cc), lambda: act_far(copy), lambda: act_here(local))
+
+                pl.when(zhi == px if h < 2 else core == yhi)(act)
+
+    x_each(lambda copy: copy.start(), lambda copy: copy.start())
+
     lane6 = lanes_of((6, LANES))
     mload.wait()
     for a in range(2):
@@ -130,37 +161,6 @@
             left = m_ref[:, a, pl.ds(LANES * max(t - 1, 0), LANES)]
             msh[t, a, :, :LANES] = here
             msh[t, a, :, LANES:] = jnp.where(lane6 < 64, right, left)
-
-    pad[...] = jnp.zeros_like(pad)
-    img[...] = jnp.zeros_like(img)
-    xload.wait()
-    pl.semaphore_wait(barrier, 15 + 6 + 4 + 8 - 2 * mine)
-
-    near = turn(zhi, 3 + 2 * zlo, 4)
-    served = ((zhi, zlo), (near, 0), (near, 1), (turn(zhi, 2, 4), 1 - zlo))
-
-    def x_each(act_far, act_here):
-        for to, (to_hi, to_lo) in enumerate(served):
-            for h in range(3):
-                cc = 4 * to_hi + 2 * to_lo + (1 if h < 2 else 0)
-                half = h if h < 2 else ylo
-                k = 4 * zhi + 2 * core + half
-                src = xv.at[pl.ds(3 * half, SLICES), :, pl.ds(pl.multiple_of(LANES * cc, LANES), LANES)]
-                copy = rcopy(src, xbuf.at[k], x_send.at[to, h], ag_recv.at[0, k], col_dev(cc))
-                local = pltpu.make_async_copy(src, xbuf.at[k], ag_recv.at[0, k])
-
-                def act(copy=copy, local=local, cc=cc):
-                    apart(col_dev(cc), lambda: act_far(copy), lambda: act_here(local))
-
-                pl.when(zhi == px if h < 2 else core == yhi)(act)
-
-    x_each(lambda copy: copy.start(), lambda copy: copy.start())
-
-    tabs = []
-    for n, (src, dst, _) in enumerate(tables):
-        t = rcopy(src, dst.at[zlo], tab_send.at[n], tab_recv.at[n], partner)
-        t.start()
-        tabs.append(t)
 
     def m_copy(d):
         k = turn(c, d, PIECES)
@@ -234,6 +234,9 @@
                     acc = acc + pad[SLICES * a + s, t, pl.ds(LINES - rs, ROWS), :]
                 img[a, t] = acc
 
+    def smem_copy(n):
+        return pltpu.make_async_copy(tables[n][1], tables[n][2].at[1 - zlo], tab_loc.at[n])
+
     def gather_project(buf, halo, n, during):
         for da in (0, 1, 3, 2):
             k = pid(turn(u, 4 - da, 4), w)
@@ -243,6 +246,11 @@
                 gather_copy2(buf, n, da, d).start()
             halo_start(buf, halo, n, k)
 
+        if n == 0:
+            for i in range(3):
+                tabs[i].wait()
+                smem_copy(i).start()
+
         @pl.loop(0, 8)
         def _(t):
             k = pid(turn(u, 4 - step(lax.div(t, 2)), 4), turn(w, 3 - 2 * lax.rem(t, 2), 4))
@@ -251,6 +259,9 @@
 
         if n == 0:
             m_start()
+            for i in range(3):
+                smem_copy(i).wait()
+                table_copy(i).wait()
 
         @pl.loop(0, PIECES)
         def _(t):
@@ -464,16 +475,6 @@
         @pl.loop(0, 12)
         def _(t):
             rcopy(src.at[0], land1.at[0, 0], rs_send.at[n, t], rs_recv.at[n, 0], partner).wait_send()
-
-    def smem_copy(n):
-        return pltpu.make_async_copy(tables[n][1], tables[n][2], loc_sem.at[4 + n])
-
-    for n in range(3):
-        table_copy(n).wait()
-        tabs[n].wait()
-        smem_copy(n).start()
-    for n in range(3):
-        smem_copy(n).wait()
 
     def place_measured():
         @pl.loop(1, PIECES)
@@ -632,7 +633,7 @@
         vmem((6, 2, X), F32),
         vmem((PIECES, 2, 6, 2 * LANES), F32),
         vmem((PIECES, 2, 6, 2 * LANES), F32),
-        vmem((2, 2, 48), jnp.int32), vmem((2, 2, 48), jnp.int32), vmem((2, 2, 48), F32),
+        vmem((2, 48), jnp.int32), vmem((2, 48), jnp.int32), vmem((2, 48), F32),
         pltpu.SMEM((2, 2, 48), jnp.int32), pltpu.SMEM((2, 2, 48), jnp.int32), pltpu.SMEM((2, 2, 48), F32),
         vmem((PIECES,) + piece, F32), vmem((PIECES, 2) + piece, F32),
         vmem((PIECES,) + piece, F32), vmem((PIECES, 2) + piece, F32),
@@ -645,7 +646,7 @@
         vmem((PIECES, 2, 6, LANES), F32), vmem((PIECES, 2, 6, LANES), F32),
         vmem(measured.shape, F32), vmem(measured.shape, F32),
         vmem((2, 3, 8, LANES), F32), vmem((2, PIECES, 8, LANES), F32), vmem((2, 4, 8, LANES), F32), vmem((2, 4, 8, LANES), F32),
-        dma((8,)), dma((3,)), dma((3,)), dma((PIECES,)), dma((PIECES,)), dma((4, 3)),
+        dma((8,)), dma((3,)), dma((3,)), dma((3,)), dma((PIECES,)), dma((PIECES,)), dma((4, 3)),
         dma((2, 15)), dma((2, PIECES)), dma((2, 2, PIECES)), dma((2, 2, PIECES)),
         dma((2, 12)), dma((2, 12)), dma((1, 3)), dma((1, 3)), dma((4,)), dma((4,)),
         dma((2, 32)), dma((2, 32)), dma((2, PIECES)), dma((2, PIECES)), dma((2, 3, PIECES)), dma((2, 3, PIECES)), dma((2, 6)),

time: 104 us -> 104 us (level)
  no operation moved by 1% of the time
where the time goes in v6:
time: 104 us
  Pallas kernels  99.2 us (95%)
  local copies, waits for them, and re-layouts  4.15 us (4%)
    pallas_call x1, Pallas kernels, per_device(): pl.pallas_call(kernel, out_shape=(jax.ShapeDtypeStruct(start_volume.shape...  99.2 us
    unnamed x7, local copies, waits for them, and re-layouts  4.15 us

profile of v6, /device:TPU:1, one launch (start us, length us, event | category | flops | bytes accessed | tf_op | source)
XLA Modules:
  0.0 104.0 jit_solution(15782925022033740178)
XLA Ops:
  0.6 99.2 %shard_map.76 = (f32[6,24,2048]{2,1,0:T(8,128)}, f32[6,2,2048]{2,1,0:T(2,128)}, f32[6,24,2048]{2,1,0:T(8,128)}) custom-call(f32[6,24,2048]{2,1,0:T(8,128)} %x_hbm.1, f32[6,2,2048]{2,1,0:T(2,128)} %bitcast.2, s32[2,48]{1,0:T(2,128)} %rt_ref.1, s32[2,48]{1,0:T(2,128)} %ct_ref.1, f32[2,48]{1,0:T(2,128)} %ft_ref.1), custom_call_target="tpu_custom_call" | custom-call | tf_op jit(solution)/shard_map/pallas_call | solution.py:657
  99.9 0.0 copy-start.1
  99.9 0.0 copy-start
  99.9 2.5 %copy.11 = f32[6,24,2048]{2,1,0:T(8,128)} copy(f32[6,24,2048]{2,1,0:T(8,128)} %get-tuple-element.12) | data formatting | bytes 2359296
  102.4 0.0 copy-done.1
  102.4 0.6 copy.12
  103.0 0.0 copy-done
  103.0 1.0 copy.13
Async XLA Ops:
  99.9 2.5 %copy-start.1 = (f32[6,2,2048]{2,1,0:T(2,128)S(1)}, f32[6,2,2048]{2,1,0:T(2,128)}, u32[]{:S(2)}) copy-start(f32[6,2,2048]{2,1,0:T(2,128)} %get-tuple-element.7) | copy-start | bytes 294916
  99.9 3.1 %copy-start = (f32[6,24,2048]{2,1,0:T(8,128)S(1)}, f32[6,24,2048]{2,1,0:T(8,128)}, u32[]{:S(2)}) copy-start(f32[6,24,2048]{2,1,0:T(8,128)} %get-tuple-element.14) | copy-start | bytes 3538948

commit v7 on v6

--- a/solution.py
+++ b/solution.py
@@ -32,7 +32,7 @@
     xv, volv, dirv, gslab, qslab, m_ref, msh, mbuf, rtv, ctv, ftv, rts, cts, fts,
     xbuf, xhalo, gbuf, ghalo, pad, img, wide, diff,
     part, rs1, sum1, rs2, own, qpart, qrs1, qsum1, qland,
-    rblk, iblk, rres, ires, tiles, sc1, sc2, sc3,
+    rows_out, rows_in, tiles, sc1, sc2, sc3,
     loc_sem, tab_send, tab_recv, tab_loc, m_send, m_recv, x_send,
     ag_send, ag_recv, hl_send, hl_recv,
     rs_send, rs_recv, rt_send, rt_recv, own_send, own_recv,
@@ -121,8 +121,16 @@
     xload = pltpu.make_async_copy(x_hbm, xv, loc_sem.at[1])
     xload.start()
 
-    pad[...] = jnp.zeros_like(pad)
-    img[...] = jnp.zeros_like(img)
+    lane6 = lanes_of((6, LANES))
+    mload.wait()
+    for a in range(2):
+        for t in range(PIECES):
+            here = m_ref[:, a, pl.ds(LANES * t, LANES)]
+            right = m_ref[:, a, pl.ds(LANES * min(t + 1, 15), LANES)]
+            left = m_ref[:, a, pl.ds(LANES * max(t - 1, 0), LANES)]
+            msh[t, pl.ds(6 * a, 6), :] = here
+            msh[t, pl.ds(12 + 6 * a, 6), :] = jnp.where(lane6 < 64, right, left)
+
     xload.wait()
     pl.semaphore_wait(barrier, 15 + 6 + 4 + 8 - 2 * mine)
 
@@ -152,26 +160,18 @@
 
     x_each(lambda copy: copy.start(), lambda copy: copy.start())
 
-    lane6 = lanes_of((6, LANES))
-    mload.wait()
-    for a in range(2):
-        for t in range(PIECES):
-            here = m_ref[:, a, pl.ds(LANES * t, LANES)]
-            right = m_ref[:, a, pl.ds(LANES * min(t + 1, 15), LANES)]
-            left = m_ref[:, a, pl.ds(LANES * max(t - 1, 0), LANES)]
-            msh[t, a, :, :LANES] = here
-            msh[t, a, :, LANES:] = jnp.where(lane6 < 64, right, left)
-
     def m_copy(d):
         k = turn(c, d, PIECES)
         return rcopy(msh.at[k], mbuf.at[c], m_send.at[d], m_recv.at[c], col_dev(k))
 
-    def m_start():
-        @pl.loop(1, PIECES)
-        def _(d):
-            m_copy(d).start()
+    @pl.loop(1, PIECES)
+    def _(d):
+        m_copy(d).start()
 
     mbuf[c] = msh[c]
+
+    pad[...] = jnp.zeros_like(pad)
+    img[...] = jnp.zeros_like(img)
 
     def step(q):
         return jnp.where(q < 2, q, 5 - q)
@@ -258,7 +258,6 @@
             halo_start(buf, halo, n, k)
 
         if n == 0:
-            m_start()
             for i in range(3):
                 smem_copy(i).wait()
                 table_copy(i).wait()
@@ -372,11 +371,8 @@
             copy = owner_copy(a, total1, land)
             pl.when(jnp.logical_not(is_me(owner_dev(*xy(a, w)))))(lambda: copy.wait_send())
 
-    def slab_at(buf, h, block):
-        return buf.at[pl.ds(3 * h, SLICES), :, pl.ds(pl.multiple_of(LANES * block, LANES), LANES)]
-
     def slab_piece(buf, xx, yy, lo):
-        return slab_at(buf, lax.rem(yy, 2), 4 * xx + 2 * lo + lax.div(yy, 2))
+        return buf.at[2 * (4 * xx + yy) + lo]
 
     def slab_copy(buf, n, a, b, lo, slot, dev):
         xx, yy = xy(a, b)
@@ -390,11 +386,11 @@
         slab_copy(buf, n, a, b, lo, 0, partner).wait_recv()
 
     def swap_copy(src, buf, n):
-        return rcopy(src, slab_at(buf, ylo, c), sl_send.at[n, 31],
+        return rcopy(src, slab_piece(buf, zhi, 2 * core + ylo, zlo), sl_send.at[n, 31],
                      sl_recv.at[n, 2 * (4 * zhi + 2 * core + ylo) + zlo], owner_dev(px, py))
 
     def swap_start(src, buf, n):
-        local = pltpu.make_async_copy(src, slab_at(buf, ylo, c), sl_recv.at[n, 2 * (4 * zhi + 2 * core + ylo) + zlo])
+        local = pltpu.make_async_copy(src, slab_piece(buf, zhi, 2 * core + ylo, zlo), sl_recv.at[n, 2 * (4 * zhi + 2 * core + ylo) + zlo])
         apart(owner_dev(px, py), lambda: swap_copy(src, buf, n).start(), lambda: local.start())
 
     def slab_near(buf, n, a, lo, slot):
@@ -438,25 +434,23 @@
         def _(t):
             slab_copy(buf, n, u, w, zlo, t, partner).wait_send()
 
-    def blk_copy(src, dst, n, d):
+    def blk_copy(d):
         k = turn(c, d, PIECES)
-        return rcopy(src.at[k], dst.at[:, :, pl.ds(pl.multiple_of(LANES * c, LANES), LANES)], blk_send.at[n, d],
-                     blk_recv.at[n, c], col_dev(k))
-
-    def blk_send_all(src, dst, n):
+        return rcopy(rows_out.at[k], rows_in.at[c], blk_send.at[d], blk_recv.at[c], col_dev(k))
+
+    def blk_start():
         @pl.loop(1, PIECES)
         def _(d):
-            blk_copy(src, dst, n, d).start()
-
-        dst[:, :, pl.ds(pl.multiple_of(LANES * c, LANES), LANES)] = src[c]
-
-    def blk_finish(src, dst, n):
+            blk_copy(d).start()
+
+        rows_in[c] = rows_out[c]
+
+    def blk_finish():
         @pl.loop(1, PIECES)
         def _(d):
             k = turn(c, d, PIECES)
-            rcopy(src.at[0], dst.at[:, :, pl.ds(pl.multiple_of(LANES * k, LANES), LANES)], blk_send.at[n, d],
-                  blk_recv.at[n, k], partner).wait_recv()
-            blk_copy(src, dst, n, d).wait_send()
+            rcopy(rows_out.at[0], rows_in.at[k], blk_send.at[d], blk_recv.at[k], partner).wait_recv()
+            blk_copy(d).wait_send()
 
     def gather_finish(buf, halo, n):
         if n:
@@ -486,13 +480,13 @@
             rows = pl.ds(6 * (2 * (k // 4) + k % 2), 6)
             for e in range(2):
                 for t in range(2):
-                    wide[2 * ((k // 2) % 2) + e, t, rows, :] = mbuf[k, e, :, LANES * t:LANES * (t + 1)]
-
-    def rows_of(blk):
+                    wide[2 * ((k // 2) % 2) + e, t, rows, :] = mbuf[k, pl.ds(12 * t + 6 * e, 6), :]
+
+    def rows_of(kind):
         for k in range(PIECES):
             rows = pl.ds(6 * (2 * (k // 4) + k % 2), 6)
             for e in range(2):
-                blk[k, e] = wide[2 * ((k // 2) % 2) + e, 0, rows, :]
+                rows_out[k, pl.ds(12 * kind + 6 * e, 6), :] = wide[2 * ((k // 2) % 2) + e, 0, rows, :]
 
     gather_project(xbuf, xhalo, 0, place_measured)
     for a in range(ANGLES):
@@ -501,8 +495,7 @@
     make_diff()
 
     back_scatter(part, rs1, 0, turn(u, 1, 4))
-    rows_of(rblk)
-    blk_send_all(rblk, rres, 0)
+    rows_of(0)
     own[...] = plane_sum(part, rs1, sum1, rs2, 0)
     gbuf[p] = own[...]
     gather_send1(gbuf, 1)
@@ -567,7 +560,7 @@
     slab_second(gslab, 0)
     owner_start(qpart, qrs1, qsum1, qland, 1)
     sum_step(0, 0)
-    rows_of(iblk)
+    rows_of(1)
 
     @pl.loop(1, PIECES)
     def _(d):
@@ -580,11 +573,11 @@
         scatter_copy2(sum1, rs2, 0, d).wait_send()
     x_each(lambda copy: copy.wait_send(), lambda copy: None)
     q = owner_sum(qsum1, qland)
-    qslab[pl.ds(3 * ylo, SLICES), :, pl.ds(pl.multiple_of(LANES * (4 * px + 2 * zlo + yhi), LANES), LANES)] = q
+    qslab[2 * p + zlo] = q
     slab_first(qslab, 1)
     tiles[1, 0, 0:1, :] = down(jnp.sum(q * q, axis=0))
     sum_start(1, 0)
-    blk_send_all(iblk, ires, 1)
+    blk_start()
     sum_step(0, 1)
     slab_third(gslab, 0)
     slab_second(qslab, 1)
@@ -597,23 +590,35 @@
     slab_third(qslab, 1)
     sum_step(1, 1)
 
-    blk_finish(rblk, rres, 0)
-    blk_finish(iblk, ires, 1)
-    for e in range(2):
-        res_out[:, e, :] = rres[e] - alpha * ires[e]
+    blk_finish()
+    for k in range(PIECES):
+        for e in range(2):
+            at = pl.ds(LANES * k, LANES)
+            res_out[:, e, at] = rows_in[k, pl.ds(6 * e, 6), :] - alpha * rows_in[k, pl.ds(12 + 6 * e, 6), :]
 
     def out_copy(src, dst, n, i):
         return pltpu.make_async_copy(src.at[i], dst.at[i], out_sem.at[n, i])
 
+    def each_piece(h):
+        for xx in range(4):
+            for yy in (h, h + 2):
+                for lo in range(2):
+                    block = LANES * (4 * xx + 2 * lo + yy // 2)
+                    yield 2 * (4 * xx + yy) + lo, (slice(3 * h, 3 * h + 3), slice(None), slice(block, block + LANES))
+
     slab_rest(gslab, 0)
-    for i in range(6):
-        volv[i] = xv[i] + alpha * gslab[i]
-        out_copy(volv, vol_out, 0, i).start()
+    for h in range(2):
+        for k, at in each_piece(h):
+            volv[at] = xv[at] + alpha * gslab[k]
+        for i in range(3 * h, 3 * h + 3):
+            out_copy(volv, vol_out, 0, i).start()
     scale = alpha * alpha * (jnp.sum(sum_finish(1, 2), axis=1, keepdims=True)[0:1] / gamma)
     slab_rest(qslab, 1)
-    for i in range(6):
-        dirv[i] = scale * gslab[i] - alpha * qslab[i]
-        out_copy(dirv, dir_out, 1, i).start()
+    for h in range(2):
+        for k, at in each_piece(h):
+            dirv[at] = scale * gslab[k] - alpha * qslab[k]
+        for i in range(3 * h, 3 * h + 3):
+            out_copy(dirv, dir_out, 1, i).start()
 
     slab_finish(gslab, 0)
     slab_finish(qslab, 1)
@@ -629,10 +634,10 @@
     dma = pltpu.SemaphoreType.DMA
     scratch = [
         vmem(start_volume.shape, F32), vmem(start_volume.shape, F32), vmem(start_volume.shape, F32),
-        vmem(start_volume.shape, F32), vmem(start_volume.shape, F32),
+        vmem((32,) + piece, F32), vmem((32,) + piece, F32),
         vmem((6, 2, X), F32),
-        vmem((PIECES, 2, 6, 2 * LANES), F32),
-        vmem((PIECES, 2, 6, 2 * LANES), F32),
+        vmem((PIECES, 24, LANES), F32),
+        vmem((PIECES, 24, LANES), F32),
         vmem((2, 48), jnp.int32), vmem((2, 48), jnp.int32), vmem((2, 48), F32),
         pltpu.SMEM((2, 2, 48), jnp.int32), pltpu.SMEM((2, 2, 48), jnp.int32), pltpu.SMEM((2, 2, 48), F32),
         vmem((PIECES,) + piece, F32), vmem((PIECES, 2) + piece, F32),
@@ -643,13 +648,12 @@
         vmem((ANGLES, 2, ROWS, LANES), F32),
         vmem((PIECES,) + piece, F32), vmem((3, 4) + piece, F32), vmem((4,) + piece, F32), vmem((3,) + piece, F32), vmem(piece, F32),
         vmem((PIECES,) + piece, F32), vmem((3, 4) + piece, F32), vmem((4,) + piece, F32), vmem((4,) + piece, F32),
-        vmem((PIECES, 2, 6, LANES), F32), vmem((PIECES, 2, 6, LANES), F32),
-        vmem(measured.shape, F32), vmem(measured.shape, F32),
+        vmem((PIECES, 24, LANES), F32), vmem((PIECES, 24, LANES), F32),
         vmem((2, 3, 8, LANES), F32), vmem((2, PIECES, 8, LANES), F32), vmem((2, 4, 8, LANES), F32), vmem((2, 4, 8, LANES), F32),
         dma((8,)), dma((3,)), dma((3,)), dma((3,)), dma((PIECES,)), dma((PIECES,)), dma((4, 3)),
         dma((2, 15)), dma((2, PIECES)), dma((2, 2, PIECES)), dma((2, 2, PIECES)),
         dma((2, 12)), dma((2, 12)), dma((1, 3)), dma((1, 3)), dma((4,)), dma((4,)),
-        dma((2, 32)), dma((2, 32)), dma((2, PIECES)), dma((2, PIECES)), dma((2, 3, PIECES)), dma((2, 3, PIECES)), dma((2, 6)),
+        dma((2, 32)), dma((2, 32)), dma((PIECES,)), dma((PIECES,)), dma((2, 3, PIECES)), dma((2, 3, PIECES)), dma((2, 6)),
     ]
     whole = pl.BlockSpec(memory_space=pltpu.VMEM)
     far = pl.BlockSpec(memory_space=pltpu.HBM)

time: 104 us -> 105 us (level)
  no operation moved by 1% of the time
where the time goes in v7:
time: 105 us
  Pallas kernels  100 us (95%)
  local copies, waits for them, and re-layouts  4.15 us (4%)
    pallas_call x1, Pallas kernels, per_device(): pl.pallas_call(kernel, out_shape=(jax.ShapeDtypeStruct(start_volume.shape...  100 us
    unnamed x7, local copies, waits for them, and re-layouts  4.15 us

profile of v7, /device:TPU:1, one launch (start us, length us, event | category | flops | bytes accessed | tf_op | source)
XLA Modules:
  0.0 105.0 jit_solution(10718976227622576221)
XLA Ops:
  0.6 100.2 %shard_map.76 = (f32[6,24,2048]{2,1,0:T(8,128)}, f32[6,2,2048]{2,1,0:T(2,128)}, f32[6,24,2048]{2,1,0:T(8,128)}) custom-call(f32[6,24,2048]{2,1,0:T(8,128)} %x_hbm.1, f32[6,2,2048]{2,1,0:T(2,128)} %bitcast.2, s32[2,48]{1,0:T(2,128)} %rt_ref.1, s32[2,48]{1,0:T(2,128)} %ct_ref.1, f32[2,48]{1,0:T(2,128)} %ft_ref.1), custom_call_target="tpu_custom_call" | custom-call | tf_op jit(solution)/shard_map/pallas_call | solution.py:661
  100.8 0.0 copy-start.1
  100.8 0.0 copy-start
  100.9 2.5 %copy.11 = f32[6,24,2048]{2,1,0:T(8,128)} copy(f32[6,24,2048]{2,1,0:T(8,128)} %get-tuple-element.12) | data formatting | bytes 2359296
  103.3 0.0 copy-done.1
  103.3 0.6 copy.12
  104.0 0.0 copy-done
  104.0 1.0 copy.13
Async XLA Ops:
  100.8 2.5 %copy-start.1 = (f32[6,2,2048]{2,1,0:T(2,128)S(1)}, f32[6,2,2048]{2,1,0:T(2,128)}, u32[]{:S(2)}) copy-start(f32[6,2,2048]{2,1,0:T(2,128)} %get-tuple-element.7) | copy-start | bytes 294916
  100.8 3.1 %copy-start = (f32[6,24,2048]{2,1,0:T(8,128)S(1)}, f32[6,24,2048]{2,1,0:T(8,128)}, u32[]{:S(2)}) copy-start(f32[6,24,2048]{2,1,0:T(8,128)} %get-tuple-element.14) | copy-start | bytes 3538948

commit v8 on v5

--- a/solution.py
+++ b/solution.py
@@ -239,7 +239,7 @@
             k = pid(turn(u, 4 - da, 4), w)
             if n == 0 or da:
                 gather_wait(buf, n, k)
-            for d in (2, 1, 3):
+            for d in (1, 3, 2):
                 gather_copy2(buf, n, da, d).start()
             halo_start(buf, halo, n, k)
 

time: 104 us -> 104 us (level)
  no operation moved by 1% of the time
where the time goes in v8:
time: 104 us
  Pallas kernels  98.7 us (95%)
  local copies, waits for them, and re-layouts  4.15 us (4%)
    pallas_call x1, Pallas kernels, per_device(): pl.pallas_call(kernel, out_shape=(jax.ShapeDtypeStruct(start_volume.shape...  98.7 us
    unnamed x7, local copies, waits for them, and re-layouts  4.15 us

profile of v8, /device:TPU:1, one launch (start us, length us, event | category | flops | bytes accessed | tf_op | source)
XLA Modules:
  0.0 103.5 jit_solution(16713450933327708340)
XLA Ops:
  0.6 98.7 %shard_map.76 = (f32[6,24,2048]{2,1,0:T(8,128)}, f32[6,2,2048]{2,1,0:T(2,128)}, f32[6,24,2048]{2,1,0:T(8,128)}) custom-call(f32[6,24,2048]{2,1,0:T(8,128)} %x_hbm.1, f32[6,2,2048]{2,1,0:T(2,128)} %bitcast.2, s32[2,48]{1,0:T(2,128)} %rt_ref.1, s32[2,48]{1,0:T(2,128)} %ct_ref.1, f32[2,48]{1,0:T(2,128)} %ft_ref.1), custom_call_target="tpu_custom_call" | custom-call | tf_op jit(solution)/shard_map/pallas_call | solution.py:656
  99.3 0.0 copy-start.1
  99.3 0.0 copy-start
  99.4 2.5 %copy.11 = f32[6,24,2048]{2,1,0:T(8,128)} copy(f32[6,24,2048]{2,1,0:T(8,128)} %get-tuple-element.12) | data formatting | bytes 2359296
  101.8 0.0 copy-done.1
  101.8 0.6 copy.12
  102.5 0.0 copy-done
  102.5 1.0 copy.13
Async XLA Ops:
  99.3 2.5 %copy-start.1 = (f32[6,2,2048]{2,1,0:T(2,128)S(1)}, f32[6,2,2048]{2,1,0:T(2,128)}, u32[]{:S(2)}) copy-start(f32[6,2,2048]{2,1,0:T(2,128)} %get-tuple-element.7) | copy-start | bytes 294916
  99.3 3.1 %copy-start = (f32[6,24,2048]{2,1,0:T(8,128)S(1)}, f32[6,24,2048]{2,1,0:T(8,128)}, u32[]{:S(2)}) copy-start(f32[6,24,2048]{2,1,0:T(8,128)} %get-tuple-element.14) | copy-start | bytes 3538948

commit v9 on v8

--- a/solution.py
+++ b/solution.py
@@ -391,10 +391,10 @@
         slab_copy(buf, n, a, w, lo, slot + 1, second_dev(3)).start()
 
     def slab_first(buf, n):
-        for i, d in enumerate((2, 1, 3)):
+        for i, d in enumerate((1, 3, 2)):
             slab_copy(buf, n, u, w, zlo, i, plane_dev(pid(turn(u, d, 4), w))).start()
         slab_near(buf, n, u, zlo, 7)
-        for i, d in enumerate((2, 1, 3, 0)):
+        for i, d in enumerate((0, 1, 3, 2)):
             slab_copy(buf, n, u, w, zlo, 3 + i, (2 * pid(turn(u, d, 4), w) + 1 - zlo, slab)).start()
 
     def slab_second(buf, n):
@@ -563,8 +563,8 @@
     tiles[0, 0, 0:1, :] = down(jnp.sum(g * g, axis=0))
     tiles[0, 0, 1:2, :] = down(norm)
     sum_start(0, 0)
+    owner_start(qpart, qrs1, qsum1, qland, 1)
     slab_second(gslab, 0)
-    owner_start(qpart, qrs1, qsum1, qland, 1)
     sum_step(0, 0)
     rows_of(iblk)
 

time: 104 us -> 103 us (level)
  no operation moved by 1% of the time
where the time goes in v9:
time: 103 us
  Pallas kernels  97.7 us (95%)
  local copies, waits for them, and re-layouts  4.15 us (4%)
    pallas_call x1, Pallas kernels, per_device(): pl.pallas_call(kernel, out_shape=(jax.ShapeDtypeStruct(start_volume.shape...  97.7 us
    unnamed x7, local copies, waits for them, and re-layouts  4.15 us

profile of v9, /device:TPU:1, one launch (start us, length us, event | category | flops | bytes accessed | tf_op | source)
XLA Modules:
  0.0 102.5 jit_solution(11837780841732716432)
XLA Ops:
  0.6 97.7 %shard_map.76 = (f32[6,24,2048]{2,1,0:T(8,128)}, f32[6,2,2048]{2,1,0:T(2,128)}, f32[6,24,2048]{2,1,0:T(8,128)}) custom-call(f32[6,24,2048]{2,1,0:T(8,128)} %x_hbm.1, f32[6,2,2048]{2,1,0:T(2,128)} %bitcast.2, s32[2,48]{1,0:T(2,128)} %rt_ref.1, s32[2,48]{1,0:T(2,128)} %ct_ref.1, f32[2,48]{1,0:T(2,128)} %ft_ref.1), custom_call_target="tpu_custom_call" | custom-call | tf_op jit(solution)/shard_map/pallas_call | solution.py:656
  98.4 0.0 copy-start.1
  98.4 0.0 copy-start
  98.4 2.5 %copy.11 = f32[6,24,2048]{2,1,0:T(8,128)} copy(f32[6,24,2048]{2,1,0:T(8,128)} %get-tuple-element.12) | data formatting | bytes 2359296
  100.9 0.0 copy-done.1
  100.9 0.6 copy.12
  101.5 0.0 copy-done
  101.5 1.0 copy.13
Async XLA Ops:
  98.4 2.5 %copy-start.1 = (f32[6,2,2048]{2,1,0:T(2,128)S(1)}, f32[6,2,2048]{2,1,0:T(2,128)}, u32[]{:S(2)}) copy-start(f32[6,2,2048]{2,1,0:T(2,128)} %get-tuple-element.7) | copy-start | bytes 294916
  98.4 3.1 %copy-start = (f32[6,24,2048]{2,1,0:T(8,128)S(1)}, f32[6,24,2048]{2,1,0:T(8,128)}, u32[]{:S(2)}) copy-start(f32[6,24,2048]{2,1,0:T(8,128)} %get-tuple-element.14) | copy-start | bytes 3538948
